TPU v7x, 32 devices: a whole 2x2x4 slice. The times are simulated.
32 devices in a mesh: row: 4 (over x, core), col: 8 (over z, y).
Axes of the slice: x: 2, y: 2, z: 4, core: 2. Of those that a mesh axis runs over, the one named last changes fastest.
Arguments:
- blocks: bfloat16 [1536, 27, 48, 48], P(('row', 'col')), may hold values from -0.59765625 to 0.59765625
- prolong: bfloat16 [1536, 48, 48], P(('row', 'col')), may hold values from -0.875 to 0.875
- columns: int32 [1536, 27], P(('row', 'col')), may hold values from 0 to 191
- aggregate: int32 [1536], P(('row', 'col')), may hold values from 0 to 15
- slots: int32 [1536, 27], P(('row', 'col')), may hold values from 0 to 26
Outputs:
- coarse: float32 [64, 27, 2304], P('row', None, 'col')
Inputs may be any that keep to these rules, and one draw needn't show every extreme that they name: `columns`: a fine block row's neighbours all lie in its column tile: the fine block rows of the devices with the same col index, in order of their row index.
All inputs are finite; a program needn't handle non-finite values.
Results may differ from a plain program's by a relative error of at most 0.0029.
Values may be sent and summed in bfloat16 or wider, within the bound.
A program may use at most 192 MiB of HBM per device.

v0:
```python
import jax
import jax.numpy as jnp
from jax import lax
from jax.sharding import PartitionSpec as P

KC = 27
CR_SLAB = 16


def shards(blocks, prolong, columns, aggregate, slots):
    width = blocks.shape[2]
    tile = lax.all_gather(prolong, "row", axis=0, tiled=True)
    picked = jnp.take(tile, columns, axis=0)
    product = jnp.einsum(
        "rkab,rkbc->rkac", blocks, picked, preferred_element_type=jnp.float32
    ).astype(jnp.bfloat16)
    term = jnp.einsum("rba,rkbc->rkac", prolong, product, preferred_element_type=jnp.float32)
    target = (aggregate[:, None] * KC + slots).reshape(-1)
    partial_value = jax.ops.segment_sum(
        term.reshape(-1, width * width), target, num_segments=CR_SLAB * KC
    )
    partial_value = partial_value.reshape(CR_SLAB, KC, width * width)
    summed = lax.psum(partial_value, "col")
    share = width * width // lax.axis_size("col")
    result = lax.dynamic_slice_in_dim(summed, lax.axis_index("col") * share, share, 2)
    return result


def solution(mesh):
    return jax.shard_map(
        shards,
        mesh=mesh,
        in_specs=(
            P(("row", "col"), None, None, None),
            P(("row", "col"), None, None),
            P(("row", "col"), None),
            P(("row", "col")),
            P(("row", "col"), None),
        ),
        out_specs=P("row", None, "col"),
        check_vma=False,
    )
```

profile of v0, /device:TPU:0, one launch (start us, length us, event | category | flops | bytes accessed | tf_op | source)
XLA Modules:
  0.0 352.0 jit_solution(4411675080666767245)
XLA Ops:
  6.5 0.0 all-reduce.2.cloned.1.call-start
  6.5 0.7 compare_select_fusion
  7.3 0.7 compare_and_fusion
  8.0 18.8 %all_gather.3 = bf16[192,48,48]{2,1,0:T(8,128)(2,1)S(1)} all-gather(bf16[48,48,48]{2,1,0:T(8,128)(2,1)} %param.6), channel_id=1, replica_groups=mesh['row'=4,'col'=8] {'row'}, dimensions={0}, use_global_device_ids=true | all-gather | bytes 1105920 | tf_op jit(solution)/shard_map/all_gather | solution.py:12
  26.8 0.1 copy.14
  26.9 0.1 reshape.17
  27.0 8.0 %gather_fusion = bf16[1296,48,48]{2,1,0:T(8,128)(2,1)} fusion(bf16[192,48,48]{2,1,0:T(8,128)(2,1)S(1)} %all_gather.3, s32[2048]{0:T(1024)S(1)} %pad_clamp_fusion), kind=kCustom, calls=%fused_computation | custom fusion | bytes 11949120 | tf_op jit(solution)/shard_map/jit(_take)/gather | solution.py:13
  35.0 0.0 copy-start
  35.0 22.0 %copy.15 = bf16[48,27,48,48]{2,3,1,0:T(8,128)(2,1)} copy(bf16[48,27,48,48]{3,2,1,0:T(8,128)(2,1)} %bitcast.16) | data formatting | bytes 11943936 | tf_op jit(solution)/shard_map/jit(_take)/gather | solution.py:13
  57.0 0.1 copy.13
  57.1 0.0 copy-done
  57.1 27.9 %fusion.10 = f32[48,27,48,48]{2,3,1,0:T(8,128)} fusion(bf16[48,27,48,48]{3,2,1,0:T(8,128)(2,1)} %param.5, bf16[48,27,48,48]{2,3,1,0:T(8,128)(2,1)} %copy.15, pred[48,27]{1,0:T(8,128)(4,1)S(1)} %copy.13, bf16[48,48,48]{2,1,0:T(8,128)(2,1)S(1)} %copy-done), kind=kOutput, calls=%fused_computation.8 | convolution fusion | flops 579280896 | bytes 24110352 | tf_op jit(solution)/shard_map/rba,rkbc->rkac/dot_general | solution.py:17
  85.0 32.6 %copy.16 = f32[48,27,48,48]{3,2,1,0:T(8,128)} copy(f32[48,27,48,48]{2,3,1,0:T(8,128)} %fusion.10) | data formatting | bytes 23887872 | tf_op jit(solution)/shard_map/rba,rkbc->rkac/transpose | solution.py:17
  117.6 0.0 copy-start.2
  117.6 0.0 copy-start.1
  117.6 25.7 %reshape.27 = f32[1296,2304]{1,0:T(8,128)} reshape(f32[48,27,48,48]{3,2,1,0:T(8,128)} %copy.16) | data formatting | bytes 23887872 | tf_op jit(solution)/shard_map/reshape | solution.py:20
  143.3 0.0 copy-done.2
  143.3 0.0 copy-done.1
  143.3 0.1 copy.12
  143.4 0.1 reshape.25
  143.5 24.2 %scatter_custom_fusion = f32[432,2304]{1,0:T(8,128)} fusion(s32[1296]{0:T(1024)S(1)} %reshape.25, f32[1296,2304]{1,0:T(8,128)} %reshape.27, f32[]{:T(128)} %constant.9.clone.1), kind=kCustom, calls=%fused_computation.10 | custom fusion | flops 2985984 | bytes 3981824 | tf_op jit(solution)/shard_map/scatter-add | solution.py:19
  167.8 3.9 %reshape.14 = f32[16,27,2304]{2,1,0:T(8,128)} reshape(f32[432,2304]{1,0:T(8,128)} %scatter_custom_fusion) | data formatting | bytes 7962624 | tf_op jit(solution)/shard_map/reshape | solution.py:22
  171.7 0.0 all-reduce.2.cloned.1.call-update
  171.7 170.7 %all-reduce.2.cloned.1.call-done = f32[16,27,2304]{2,1,0:T(8,128)} async-done(((f32[16,27,2304]{2,1,0:T(8,128)}), f32[16,27,2304]{2,1,0:T(8,128)}) %all-reduce.2.cloned.1.call-update) | async-done | bytes 3981328 | tf_op jit(solution)/shard_map/psum | solution.py:23
  342.4 1.5 constant_dynamic-slice_fusion
  343.9 1.2 copy.17
  (3 shorter events, 0.0 us)
Async XLA Ops:
  6.5 335.9 %all-reduce.2.cloned.1.call-start = ((), (), s32[]{:S(2)}) async-start(), calls=%async_computation | async-start | bytes 9437184 | tf_op jit(solution)/shard_map/psum | solution.py:23
  35.0 22.1 %copy-start = (bf16[48,48,48]{2,1,0:T(8,128)(2,1)S(1)}, bf16[48,48,48]{2,1,0:T(8,128)(2,1)}, u32[]{:S(2)}) copy-start(bf16[48,48,48]{2,1,0:T(8,128)(2,1)} %param.6) | copy-start | bytes 663556
  117.6 25.7 %copy-start.2 = (s32[48]{0:T(128)S(1)}, s32[48]{0:T(128)}, u32[]{:S(2)}) copy-start(s32[48]{0:T(128)} %param.8) | copy-start | bytes 580
  117.6 25.7 %copy-start.1 = (s32[48,27]{0,1:T(8,128)S(1)}, s32[48,27]{0,1:T(8,128)}, u32[]{:S(2)}) copy-start(s32[48,27]{0,1:T(8,128)} %param.9) | copy-start | bytes 15556
Sparse Core Ops, SparseCore 0:
  171.8 170.5 all-reduce.1
where the time goes:
time: 354 us; the launch traced here: 352 us
  waiting for transfers between devices  171 us (48%)
  local copies, waits for them, and re-layouts  95.4 us (27%)
  matrix products  27.9 us (8%)
  other arithmetic  25.7 us (7%)
  blocking collectives  18.8 us (5%)
  between operations  13.4 us (4%)
    psum x1, waiting for transfers between devices, shards(): summed = lax.psum(partial_value, 'col')  171 us
    transpose x1, local copies, waits for them, and re-layouts, shards(): jnp.einsum('rba,rkbc->rkac', prolong, product, preferred_element_type=jnp...  32.6 us
    gather x2, local copies, waits for them, and re-layouts, shards(): picked = jnp.take(tile, columns, axis=0)  30 us
    dot_general x1, matrix products, shards(): jnp.einsum('rba,rkbc->rkac', prolong, product, preferred_element_type=jnp...  27.9 us
    reshape x1, local copies, waits for them, and re-layouts, shards(): term.reshape(-1, width * width)  25.7 us
    scatter-add x1, other arithmetic, shards(): jax.ops.segment_sum(term.reshape(-1, width * width), target, num_segments...  24.2 us
    all_gather x1, blocking collectives, shards(): tile = lax.all_gather(prolong, 'row', axis=0, tiled=True)  18.8 us
  transfers between devices with their start and end apart: 1, of which 1 were waited for; matrix products, arithmetic and copies ran while one was open for 0% of the time, Pallas kernels for 0%

commit v1 on v0

--- a/solution.py
+++ b/solution.py
@@ -1,13 +1,297 @@
+import functools
+
 import jax
 import jax.numpy as jnp
 from jax import lax
+from jax.experimental import pallas as pl
+from jax.experimental.pallas import tpu as pltpu
 from jax.sharding import PartitionSpec as P
 
 KC = 27
 CR_SLAB = 16
-
-
-def shards(blocks, prolong, columns, aggregate, slots):
+MESH = pl.DeviceIdType.MESH
+LANES = 128
+GROUPS = 4
+GROUP = 112
+ROWS_STEP = 4
+HALVES = ((0, 64), (64, 48))
+
+
+def placement(rows, source, dest):
+    row = lax.broadcasted_iota(jnp.int32, (rows, LANES), 0)
+    lane = lax.broadcasted_iota(jnp.int32, (rows, LANES), 1)
+    keep = (row - source == lane - dest) & (row >= source) & (row < source + 48)
+    return jnp.where(keep, 1.0, 0.0).astype(jnp.bfloat16)
+
+
+def move(value, matrix):
+    return jnp.dot(value, matrix, preferred_element_type=jnp.float32).astype(jnp.bfloat16)
+
+
+def gather_kernel(p_ref, out_ref, packed, send_sem, recv_sem):
+    rows, width = p_ref.shape[0], p_ref.shape[1]
+    half = rows // 2
+    me = lax.axis_index("row")
+    core, x = me % 2, me // 2
+    other = x * 2 + 1 - core
+    across = (1 - x) * 2 + core
+    diagonal = (1 - x) * 2 + 1 - core
+
+    barrier = pltpu.get_barrier_semaphore()
+    for peer in (other, across):
+        pl.semaphore_signal(barrier, inc=1, device_id={"row": peer}, device_id_type=MESH)
+
+    low = p_ref[:half].reshape(half * width, width)
+    high = p_ref[half:].reshape(half * width, width)
+    first, second = placement(width, 0, 0), placement(width, 0, 48)
+    both = jnp.dot(low, first, preferred_element_type=jnp.float32) + jnp.dot(
+        high, second, preferred_element_type=jnp.float32
+    )
+    packed[0] = both.astype(jnp.bfloat16)
+    pl.semaphore_wait(barrier, 2)
+
+    def send(source, dest, peer):
+        copy = pltpu.make_async_remote_copy(
+            src_ref=packed.at[source],
+            dst_ref=packed.at[dest],
+            send_sem=send_sem.at[dest],
+            recv_sem=recv_sem.at[dest],
+            device_id={"row": peer},
+            device_id_type=MESH,
+        )
+        copy.start()
+        return copy
+
+    def unpack(slot, owner):
+        value = packed[slot]
+        out_ref[pl.ds(owner * rows, half)] = move(value, placement(LANES, 0, 0)).reshape(half, width, LANES)
+        out_ref[pl.ds(owner * rows + half, half)] = move(value, placement(LANES, 48, 0)).reshape(half, width, LANES)
+
+    far = send(0, 2, across)
+    near = send(0, 1, other)
+    unpack(0, me)
+    near.wait_recv()
+    unpack(1, other)
+    far.wait_recv()
+    relay = send(2, 3, other)
+    unpack(2, across)
+    relay.wait_recv()
+    unpack(3, diagonal)
+    far.wait_send()
+    near.wait_send()
+    relay.wait_send()
+
+
+def gather_rows(prolong, n_row):
+    rows, width = prolong.shape[0], prolong.shape[1]
+    return pl.pallas_call(
+        gather_kernel,
+        out_shape=jax.ShapeDtypeStruct((n_row * rows, width, LANES), jnp.bfloat16),
+        in_specs=[pl.BlockSpec(memory_space=pltpu.VMEM)],
+        out_specs=pl.BlockSpec(memory_space=pltpu.VMEM),
+        scratch_shapes=[
+            pltpu.VMEM((4, rows // 2 * width, LANES), jnp.bfloat16),
+            pltpu.SemaphoreType.DMA((4,)),
+            pltpu.SemaphoreType.DMA((4,)),
+        ],
+        compiler_params=pltpu.CompilerParams(
+            collective_id=0, has_side_effects=True, vmem_limit_bytes=24 * 2**20
+        ),
+        name="gather_prolong",
+    )(prolong)
+
+
+def product_kernel(col_ref, slot_ref, agg_ref, tile_ref, own_ref, blk_ref, out_ref, acc):
+    step = pl.program_id(0)
+    width = own_ref.shape[1]
+    neighbours = blk_ref.shape[1]
+
+    @pl.when(step == 0)
+    def _():
+        @pl.loop(0, acc.shape[0] // 384)
+        def _(at):
+            acc[pl.ds(at * 384, 384), :] = jnp.zeros((384, LANES), jnp.float32)
+
+    @pl.loop(0, ROWS_STEP)
+    def _(r):
+        i = step * ROWS_STEP + r
+        turned = own_ref[i].astype(jnp.float32).T.astype(jnp.bfloat16)
+        aggregate = agg_ref[i]
+        for k in range(neighbours):
+            product = jnp.dot(
+                blk_ref[r, k], tile_ref[col_ref[i, k]], preferred_element_type=jnp.float32
+            ).astype(jnp.bfloat16)
+            term = jnp.dot(turned, product, preferred_element_type=jnp.float32)
+            base = pl.multiple_of((slot_ref[i, k] * CR_SLAB + aggregate) * width, width)
+            acc[pl.ds(base, width), :] += term
+
+    @pl.when(step == pl.num_programs(0) - 1)
+    def _():
+        lane = lax.broadcasted_iota(jnp.int32, (16, LANES), 1)
+
+        @pl.loop(0, 8 * (GROUP // 16))
+        def _(at):
+            d, s = at // (GROUP // 16), at % (GROUP // 16)
+            sums = [None] * 9
+            for q in range(GROUPS):
+                for r in range(6):
+                    start = (GROUP * q + 16 * s) * width + 6 * d + r
+                    offset = (q * 6 + r) * 48
+                    j, shift = offset // LANES, offset % LANES
+                    value = acc[pl.ds(start, 16, stride=width), :]
+                    if shift:
+                        value = pltpu.roll(value, shift, 1)
+                    over = shift + 48 - LANES
+                    if over > 0:
+                        spill = jnp.where(lane < over, value, 0.0)
+                        value = jnp.where(lane < over, 0.0, value)
+                        sums[j + 1] = spill
+                    sums[j] = value if sums[j] is None else sums[j] + value
+            for j in range(9):
+                out_ref[d, pl.ds(pl.multiple_of(16 * s, 16), 16), j * LANES:(j + 1) * LANES] = sums[j].astype(jnp.bfloat16)
+
+
+def products(tile, prolong, blocks, columns, aggregate, slots):
+    rows, neighbours, width = blocks.shape[0], blocks.shape[1], blocks.shape[2]
+    smem = pl.BlockSpec(memory_space=pltpu.SMEM)
+    vmem = pl.BlockSpec(memory_space=pltpu.VMEM)
+    flops = rows * neighbours * width**3 * 4
+    return pl.pallas_call(
+        product_kernel,
+        grid=(rows // ROWS_STEP,),
+        out_shape=jax.ShapeDtypeStruct((8, GROUP, 9 * LANES), jnp.bfloat16),
+        in_specs=[
+            smem,
+            smem,
+            smem,
+            vmem,
+            vmem,
+            pl.BlockSpec((ROWS_STEP, neighbours, width, width), lambda g: (g, 0, 0, 0)),
+        ],
+        out_specs=vmem,
+        scratch_shapes=[pltpu.VMEM((GROUPS * GROUP * width, LANES), jnp.float32)],
+        compiler_params=pltpu.CompilerParams(vmem_limit_bytes=40 * 2**20),
+        cost_estimate=pl.CostEstimate(flops=flops, bytes_accessed=20 * 2**20, transcendentals=0),
+        name="triple_products",
+    )(columns, slots, aggregate, tile, prolong, blocks)
+
+
+def scatter_kernel(x_ref, out_ref, ybuf, zsend, zbuf, own, ysend_sem, yrecv_sem, zsend_sem, zrecv_sem):
+    me = lax.axis_index("col")
+    y, z = me % 2, me // 2
+    partner = z * 2 + 1 - y
+    offsets = (2, 1, 3, 0)
+    targets = [(z + offset) % 4 for offset in offsets]
+
+    barrier = pltpu.get_barrier_semaphore()
+    for peer in [partner] + [t * 2 + y for t in targets[:3]]:
+        pl.semaphore_signal(barrier, inc=1, device_id={"col": peer}, device_id_type=MESH)
+    pl.semaphore_wait(barrier, 4)
+
+    ycopies, zcopies = {}, {}
+    for s in range(4):
+        for h, (begin, size) in enumerate(HALVES):
+            copy = pltpu.make_async_remote_copy(
+                src_ref=x_ref.at[targets[s] * 2 + 1 - y, pl.ds(begin, size)],
+                dst_ref=ybuf.at[s, pl.ds(begin, size)],
+                send_sem=ysend_sem.at[s, h],
+                recv_sem=yrecv_sem.at[s, h],
+                device_id={"col": partner},
+                device_id_type=MESH,
+            )
+            copy.start()
+            ycopies[s, h] = copy
+
+    for s in range(4):
+        for h, (begin, size) in enumerate(HALVES):
+            ycopies[s, h].wait_recv()
+
+            @pl.loop(begin // 16, (begin + size) // 16)
+            def _(at):
+                rows = pl.ds(pl.multiple_of(at * 16, 16), 16)
+                total = x_ref[targets[s] * 2 + y, rows, :].astype(jnp.float32) + ybuf[s, rows, :].astype(jnp.float32)
+                if s < 3:
+                    zsend[s, rows, :] = total.astype(jnp.bfloat16)
+                else:
+                    own[rows, :] = total
+
+            if s < 3:
+                copy = pltpu.make_async_remote_copy(
+                    src_ref=zsend.at[s, pl.ds(begin, size)],
+                    dst_ref=zbuf.at[s, pl.ds(begin, size)],
+                    send_sem=zsend_sem.at[s, h],
+                    recv_sem=zrecv_sem.at[s, h],
+                    device_id={"col": targets[s] * 2 + y},
+                    device_id_type=MESH,
+                )
+                copy.start()
+                zcopies[s, h] = copy
+
+    for copy in zcopies.values():
+        copy.wait_recv()
+
+    lane = lax.broadcasted_iota(jnp.int32, (16, LANES), 1)
+
+    def unpack(at, groups):
+        rows = pl.ds(pl.multiple_of(at * 16, 16), 16)
+        total = own[rows, :]
+        for s in range(3):
+            total = total + zbuf[s, rows, :].astype(jnp.float32)
+        for q in range(groups):
+            j, shift = 288 * q // LANES, 288 * q % LANES
+            turned = [total[:, (j + m) * LANES:(j + m + 1) * LANES] for m in range(3)]
+            if shift:
+                turned = [pltpu.roll(piece, LANES - shift, 1) for piece in turned]
+            target = pl.ds(pl.multiple_of(GROUP * q + at * 16, 16), 16)
+            for m in range(2):
+                piece = turned[m]
+                if shift:
+                    piece = jnp.where(lane < LANES - shift, piece, turned[m + 1])
+                out_ref[target, m * LANES:(m + 1) * LANES] = piece
+            out_ref[target, 256:288] = turned[2][:, :32]
+
+    @pl.loop(0, 6)
+    def _(at):
+        unpack(at, 4)
+
+    unpack(6, 3)
+
+    for copy in list(ycopies.values()) + list(zcopies.values()):
+        copy.wait_send()
+
+
+def scatter_cols(packed):
+    half = len(HALVES)
+    return pl.pallas_call(
+        scatter_kernel,
+        out_shape=jax.ShapeDtypeStruct((KC * CR_SLAB, 288), jnp.float32),
+        in_specs=[pl.BlockSpec(memory_space=pltpu.VMEM)],
+        out_specs=pl.BlockSpec(memory_space=pltpu.VMEM),
+        scratch_shapes=[
+            pltpu.VMEM((4, GROUP, 9 * LANES), jnp.bfloat16),
+            pltpu.VMEM((3, GROUP, 9 * LANES), jnp.bfloat16),
+            pltpu.VMEM((3, GROUP, 9 * LANES), jnp.bfloat16),
+            pltpu.VMEM((GROUP, 9 * LANES), jnp.float32),
+            pltpu.SemaphoreType.DMA((4, half)),
+            pltpu.SemaphoreType.DMA((4, half)),
+            pltpu.SemaphoreType.DMA((3, half)),
+            pltpu.SemaphoreType.DMA((3, half)),
+        ],
+        compiler_params=pltpu.CompilerParams(
+            collective_id=1, has_side_effects=True, vmem_limit_bytes=24 * 2**20
+        ),
+        name="scatter_cols",
+    )(packed)
+
+
+def shards(n_row, blocks, prolong, columns, aggregate, slots):
+    tile = gather_rows(prolong, n_row)
+    packed = products(tile, prolong, blocks, columns, aggregate, slots)
+    result = scatter_cols(packed)
+    return result.reshape(KC, CR_SLAB, 288).transpose(1, 0, 2)
+
+
+def shards_any(blocks, prolong, columns, aggregate, slots):
     width = blocks.shape[2]
     tile = lax.all_gather(prolong, "row", axis=0, tiled=True)
     picked = jnp.take(tile, columns, axis=0)
@@ -22,13 +306,14 @@
     partial_value = partial_value.reshape(CR_SLAB, KC, width * width)
     summed = lax.psum(partial_value, "col")
     share = width * width // lax.axis_size("col")
-    result = lax.dynamic_slice_in_dim(summed, lax.axis_index("col") * share, share, 2)
-    return result
+    return lax.dynamic_slice_in_dim(summed, lax.axis_index("col") * share, share, 2)
 
 
 def solution(mesh):
+    n_row, n_col = mesh.shape["row"], mesh.shape["col"]
+    body = functools.partial(shards, n_row) if (n_row, n_col) == (4, 8) else shards_any
     return jax.shard_map(
-        shards,
+        body,
         mesh=mesh,
         in_specs=(
             P(("row", "col"), None, None, None),

time: 354 us -> 87.9 us (0.25)
  waiting for transfers between devices: 171 us -> 0 us
  local copies, waits for them, and re-layouts: 95.4 us -> 3.52 us
  Pallas kernels: 0 us -> 84 us
  matrix products: 27.9 us -> 0 us
  other arithmetic: 25.7 us -> 0 us
  blocking collectives: 18.8 us -> 0 us
  between operations: 13.4 us -> 0.04 us
    psum x1 -> x0, waiting for transfers between devices: 171 us -> none  [shards(): summed = lax.psum(partial_value, 'col')]
    pallas_call x0 -> x3, Pallas kernels: none -> 84 us  [the longest x1 38.3 us: products(): pl.pallas_call(product_kernel, grid=(rows // ROWS_STEP,), out_shape=jax.S...]
    transpose x1 -> x0, local copies, waits for them, and re-layouts: 32.6 us -> none  [shards(): jnp.einsum('rba,rkbc->rkac', prolong, product, preferred_element_type=jnp...]
    gather x2 -> x0, local copies, waits for them, and re-layouts: 30 us -> none  [shards(): picked = jnp.take(tile, columns, axis=0)]
    reshape x2 -> x0, local copies, waits for them, and re-layouts: 29.6 us -> none  [the longest x1 25.7 us: shards(): term.reshape(-1, width * width)]
    dot_general x1 -> x0, matrix products: 27.9 us -> none  [shards(): jnp.einsum('rba,rkbc->rkac', prolong, product, preferred_element_type=jnp...]
    scatter-add x1 -> x0, other arithmetic: 24.2 us -> none  [shards(): jax.ops.segment_sum(term.reshape(-1, width * width), target, num_segments...]
    all_gather x1 -> x0, blocking collectives: 18.8 us -> none  [shards(): tile = lax.all_gather(prolong, 'row', axis=0, tiled=True)]
  transfers between devices with their start and end apart: 1 -> 0, of which waited for: 1 -> 0; matrix products, arithmetic and copies ran while one was open for 0% -> 0% of each run, Pallas kernels for 0% -> 0%
where the time goes in v1:
time: 87.9 us; the launch traced here: 87.6 us
  Pallas kernels  84 us (96%)
  local copies, waits for them, and re-layouts  3.52 us (4%)
    pallas_call x1, Pallas kernels, products(): pl.pallas_call(product_kernel, grid=(rows // ROWS_STEP,), out_shape=jax.S...  38.3 us
    pallas_call x1, Pallas kernels, scatter_cols(): pl.pallas_call(scatter_kernel, out_shape=jax.ShapeDtypeStruct((KC * CR_SL...  33.8 us
    pallas_call x1, Pallas kernels, gather_rows(): pl.pallas_call(gather_kernel, out_shape=jax.ShapeDtypeStruct((n_row * row...  11.9 us
    unnamed x9, local copies, waits for them, and re-layouts  3.52 us

profile of v1, /device:TPU:0, one launch (start us, length us, event | category | flops | bytes accessed | tf_op | source)
XLA Modules:
  0.0 87.6 jit_solution(5531957762094681440)
XLA Ops:
  0.0 0.0 copy-start.2
  0.0 0.8 copy.6.col_ref
  0.8 0.8 copy.7.slot_ref
  1.6 0.0 copy-start
  1.6 1.1 %copy-done = bf16[48,48,48]{2,1,0:T(8,128)(2,1)S(1)} copy-done((bf16[48,48,48]{2,1,0:T(8,128)(2,1)S(1)}, bf16[48,48,48]{2,1,0:T(8,128)(2,1)}, u32[]{:S(2)}) %copy-start) | copy-done | bytes 221208
  2.7 0.0 copy-start.1
  2.7 11.9 %gather_prolong.1.tile_ref = bf16[192,48,128]{2,1,0:T(8,128)(2,1)S(1)} custom-call(bf16[48,48,48]{2,1,0:T(8,128)(2,1)S(1)} %copy-done), custom_call_target="tpu_custom_call" | custom-call | tf_op jit(solution)/shard_map/gather_prolong/pallas_call | solution.py:87
  14.6 0.0 copy-done.2
  14.6 0.0 copy-done.1
  14.6 38.3 %triple_products.1.x_ref = bf16[8,112,1152]{2,1,0:T(8,128)(2,1)S(1)} custom-call(s32[48,27]{1,0:T(8,128)S(1)} %copy.6.col_ref, s32[48,27]{1,0:T(8,128)S(1)} %copy.7.slot_ref, s32[48]{0:T(128)S(1)} %copy-done.2, bf16[192,48,128]{2,1,0:T(8,128)(2,1)S(1)} %gather_prolong.1.tile_ref, bf16[48,48,48]{2,1,0:T(8,128)(2,1)S(1)} %copy-done.1, ...), custom_call_target="tpu_custom_call" | custom-call | flops 573308928 | bytes 20971520 | tf_op jit(solution)/shard_map/triple_products/pallas_call | solution.py:159
  52.9 33.8 %scatter_cols.1 = f32[432,288]{1,0:T(8,128)S(1)} custom-call(bf16[8,112,1152]{2,1,0:T(8,128)(2,1)S(1)} %triple_products.1.x_ref), custom_call_target="tpu_custom_call" | custom-call | tf_op jit(solution)/shard_map/scatter_cols/pallas_call | solution.py:265
  86.7 0.8 copy.9
Async XLA Ops:
  0.0 14.6 %copy-start.2 = (s32[48]{0:T(128)S(1)}, s32[48]{0:T(128)}, u32[]{:S(2)}) copy-start(s32[48]{0:T(128)} %agg_ref.1) | copy-start | bytes 580
  1.6 1.1 %copy-start = (bf16[48,48,48]{2,1,0:T(8,128)(2,1)S(1)}, bf16[48,48,48]{2,1,0:T(8,128)(2,1)}, u32[]{:S(2)}) copy-start(bf16[48,48,48]{2,1,0:T(8,128)(2,1)} %own_ref.1) | copy-start | bytes 663556
  2.7 11.9 %copy-start.1 = (bf16[48,48,48]{2,1,0:T(8,128)(2,1)S(1)}, bf16[48,48,48]{2,1,0:T(8,128)(2,1)}, u32[]{:S(2)}) copy-start(bf16[48,48,48]{2,1,0:T(8,128)(2,1)} %own_ref.1) | copy-start | bytes 663556

commit v2 on v1

--- a/solution.py
+++ b/solution.py
@@ -64,8 +64,10 @@
 
     def unpack(slot, owner):
         value = packed[slot]
-        out_ref[pl.ds(owner * rows, half)] = move(value, placement(LANES, 0, 0)).reshape(half, width, LANES)
-        out_ref[pl.ds(owner * rows + half, half)] = move(value, placement(LANES, 48, 0)).reshape(half, width, LANES)
+        for side in range(2):
+            for part in range(2):
+                piece = move(value, placement(LANES, 48 * part, 64 * side))
+                out_ref[side, pl.ds(owner * rows + half * part, half)] = piece.reshape(half, width, LANES)
 
     far = send(0, 2, across)
     near = send(0, 1, other)
@@ -86,7 +88,7 @@
     rows, width = prolong.shape[0], prolong.shape[1]
     return pl.pallas_call(
         gather_kernel,
-        out_shape=jax.ShapeDtypeStruct((n_row * rows, width, LANES), jnp.bfloat16),
+        out_shape=jax.ShapeDtypeStruct((2, n_row * rows, width, LANES), jnp.bfloat16),
         in_specs=[pl.BlockSpec(memory_space=pltpu.VMEM)],
         out_specs=pl.BlockSpec(memory_space=pltpu.VMEM),
         scratch_shapes=[
@@ -117,13 +119,24 @@
         i = step * ROWS_STEP + r
         turned = own_ref[i].astype(jnp.float32).T.astype(jnp.bfloat16)
         aggregate = agg_ref[i]
-        for k in range(neighbours):
+        blank = jnp.zeros((width, LANES), jnp.bfloat16)
+        for first in range(0, neighbours, 4):
+            group = range(first, min(first + 4, neighbours))
+            left = jnp.concatenate([blk_ref[r, k] for k in group], axis=1)
+            picked = [tile_ref[k % 4 % 2, col_ref[k, i]] for k in group]
+            picked = [
+                jnp.concatenate([p, blank] if at < 2 else [blank, p], axis=1) for at, p in enumerate(picked)
+            ]
             product = jnp.dot(
-                blk_ref[r, k], tile_ref[col_ref[i, k]], preferred_element_type=jnp.float32
+                left, jnp.concatenate(picked, axis=0), preferred_element_type=jnp.float32
             ).astype(jnp.bfloat16)
             term = jnp.dot(turned, product, preferred_element_type=jnp.float32)
-            base = pl.multiple_of((slot_ref[i, k] * CR_SLAB + aggregate) * width, width)
-            acc[pl.ds(base, width), :] += term
+            for at, k in enumerate(group):
+                value = term[:, at // 2 * LANES:(at // 2 + 1) * LANES]
+                if at % 2:
+                    value = pltpu.roll(value, 64, 1)
+                base = pl.multiple_of((slot_ref[k, i] * CR_SLAB + aggregate) * width, width)
+                acc[pl.ds(base, width), :] += value
 
     @pl.when(step == pl.num_programs(0) - 1)
     def _():
@@ -141,12 +154,9 @@
                     value = acc[pl.ds(start, 16, stride=width), :]
                     if shift:
                         value = pltpu.roll(value, shift, 1)
-                    over = shift + 48 - LANES
-                    if over > 0:
-                        spill = jnp.where(lane < over, value, 0.0)
-                        value = jnp.where(lane < over, 0.0, value)
-                        sums[j + 1] = spill
-                    sums[j] = value if sums[j] is None else sums[j] + value
+                    sums[j] = jnp.where(lane < shift, sums[j], value) if shift else value
+                    if shift + 48 > LANES:
+                        sums[j + 1] = value
             for j in range(9):
                 out_ref[d, pl.ds(pl.multiple_of(16 * s, 16), 16), j * LANES:(j + 1) * LANES] = sums[j].astype(jnp.bfloat16)
 
@@ -173,7 +183,7 @@
         compiler_params=pltpu.CompilerParams(vmem_limit_bytes=40 * 2**20),
         cost_estimate=pl.CostEstimate(flops=flops, bytes_accessed=20 * 2**20, transcendentals=0),
         name="triple_products",
-    )(columns, slots, aggregate, tile, prolong, blocks)
+    )(columns.T, slots.T, aggregate, tile, prolong, blocks)
 
 
 def scatter_kernel(x_ref, out_ref, ybuf, zsend, zbuf, own, ysend_sem, yrecv_sem, zsend_sem, zrecv_sem):

time: 87.9 us -> 114 us (1.30)
  Pallas kernels: 84 us -> 112 us
  local copies, waits for them, and re-layouts: 3.52 us -> 1.93 us
    pallas_call x1, Pallas kernels: 38.3 us -> 65.9 us  [products(): pl.pallas_call(product_kernel, grid=(rows // ROWS_STEP,), out_shape=jax.S...]
    unnamed x9 -> x11, local copies, waits for them, and re-layouts: 3.52 us -> 1.93 us
where the time goes in v2:
time: 114 us
  Pallas kernels  112 us (98%)
  local copies, waits for them, and re-layouts  1.93 us (2%)
    pallas_call x1, Pallas kernels, products(): pl.pallas_call(product_kernel, grid=(rows // ROWS_STEP,), out_shape=jax.S...  65.9 us
    pallas_call x1, Pallas kernels, scatter_cols(): pl.pallas_call(scatter_kernel, out_shape=jax.ShapeDtypeStruct((KC * CR_SL...  34.1 us
    pallas_call x1, Pallas kernels, gather_rows(): pl.pallas_call(gather_kernel, out_shape=jax.ShapeDtypeStruct((2, n_row *...  11.9 us

profile of v2, /device:TPU:0, one launch (start us, length us, event | category | flops | bytes accessed | tf_op | source)
XLA Modules:
  0.0 113.9 jit_solution(592897044826021677)
XLA Ops:
  0.0 0.0 copy-start.4
  0.0 0.0 copy-start
  0.0 1.1 copy-done
  1.1 0.0 copy-start.1
  1.1 0.0 copy-start.2
  1.1 0.0 copy-start.3
  1.1 11.9 %gather_prolong.1.tile_ref = bf16[2,192,48,128]{3,2,1,0:T(8,128)(2,1)S(1)} custom-call(bf16[48,48,48]{2,1,0:T(8,128)(2,1)S(1)} %copy-done), custom_call_target="tpu_custom_call" | custom-call | tf_op jit(solution)/shard_map/gather_prolong/pallas_call | solution.py:89
  13.0 0.0 copy-done.4
  13.0 0.0 copy-done.1
  13.0 0.0 copy-done.2
  13.0 0.0 copy-done.3
  13.0 65.9 %triple_products.1.x_ref = bf16[8,112,1152]{2,1,0:T(8,128)(2,1)S(1)} custom-call(s32[27,48]{1,0:T(8,128)S(1)} %bitcast.6, s32[27,48]{1,0:T(8,128)S(1)} %bitcast.7, s32[48]{0:T(128)S(1)} %copy-done.4, bf16[2,192,48,128]{3,2,1,0:T(8,128)(2,1)S(1)} %gather_prolong.1.tile_ref, bf16[48,48,48]{2,1,0:T(8,128)(2,1)S(1)} %copy-done.1, bf16[48,27,48,48]{3,2,1,0:T(8,128)(2,1)} %blk_ref.1), custom_call_target="tpu_custom_call" | custom-call | flops 573308928 | bytes 20971520 | tf_op jit(solution)/shard_map/triple_products/pallas_call | solution.py:169
  78.9 34.1 %scatter_cols.1 = f32[432,288]{1,0:T(8,128)S(1)} custom-call(bf16[8,112,1152]{2,1,0:T(8,128)(2,1)S(1)} %triple_products.1.x_ref), custom_call_target="tpu_custom_call" | custom-call | tf_op jit(solution)/shard_map/scatter_cols/pallas_call | solution.py:275
  113.1 0.8 copy.7
Async XLA Ops:
  0.0 13.0 %copy-start.4 = (s32[48]{0:T(128)S(1)}, s32[48]{0:T(128)}, u32[]{:S(2)}) copy-start(s32[48]{0:T(128)} %agg_ref.1) | copy-start | bytes 580
  0.0 1.1 copy-start
  1.1 11.9 %copy-start.1 = (bf16[48,48,48]{2,1,0:T(8,128)(2,1)S(1)}, bf16[48,48,48]{2,1,0:T(8,128)(2,1)}, u32[]{:S(2)}) copy-start(bf16[48,48,48]{2,1,0:T(8,128)(2,1)} %own_ref.1) | copy-start | bytes 663556
  1.1 11.9 %copy-start.2 = (s32[48,27]{0,1:T(8,128)S(1)}, s32[48,27]{0,1:T(8,128)}, u32[]{:S(2)}) copy-start(s32[48,27]{0,1:T(8,128)} %param.7) | copy-start | bytes 15556
  1.1 11.9 %copy-start.3 = (s32[48,27]{0,1:T(8,128)S(1)}, s32[48,27]{0,1:T(8,128)}, u32[]{:S(2)}) copy-start(s32[48,27]{0,1:T(8,128)} %param.9) | copy-start | bytes 15556

commit v3 on v1

--- a/solution.py
+++ b/solution.py
@@ -14,6 +14,7 @@
 GROUPS = 4
 GROUP = 112
 ROWS_STEP = 4
+PARTS = 3
 HALVES = ((0, 64), (64, 48))
 
 
@@ -112,18 +113,27 @@
         def _(at):
             acc[pl.ds(at * 384, 384), :] = jnp.zeros((384, LANES), jnp.float32)
 
-    @pl.loop(0, ROWS_STEP)
-    def _(r):
+    def one_row(r):
         i = step * ROWS_STEP + r
-        turned = own_ref[i].astype(jnp.float32).T.astype(jnp.bfloat16)
+        turned = own_ref[i]
         aggregate = agg_ref[i]
-        for k in range(neighbours):
-            product = jnp.dot(
-                blk_ref[r, k], tile_ref[col_ref[i, k]], preferred_element_type=jnp.float32
-            ).astype(jnp.bfloat16)
-            term = jnp.dot(turned, product, preferred_element_type=jnp.float32)
-            base = pl.multiple_of((slot_ref[i, k] * CR_SLAB + aggregate) * width, width)
-            acc[pl.ds(base, width), :] += term
+        for first in range(0, neighbours, 2):
+            group = range(first, min(first + 2, neighbours))
+            product = [
+                jnp.dot(
+                    blk_ref[r, k], tile_ref[col_ref[k, i]], preferred_element_type=jnp.float32
+                ).astype(jnp.bfloat16)
+                for k in group
+            ]
+            term = jnp.dot(turned, jnp.concatenate(product, axis=1), preferred_element_type=jnp.float32)
+            for at, k in enumerate(group):
+                base = pl.multiple_of((slot_ref[k, i] * CR_SLAB + aggregate) * width, width)
+                acc[pl.ds(base, width), :] += term[:, at * LANES:(at + 1) * LANES]
+
+    @pl.loop(0, ROWS_STEP // 2)
+    def _(at):
+        one_row(at * 2)
+        one_row(at * 2 + 1)
 
     @pl.when(step == pl.num_programs(0) - 1)
     def _():
@@ -151,7 +161,7 @@
                 out_ref[d, pl.ds(pl.multiple_of(16 * s, 16), 16), j * LANES:(j + 1) * LANES] = sums[j].astype(jnp.bfloat16)
 
 
-def products(tile, prolong, blocks, columns, aggregate, slots):
+def products(tile, turned, blocks, columns, aggregate, slots):
     rows, neighbours, width = blocks.shape[0], blocks.shape[1], blocks.shape[2]
     smem = pl.BlockSpec(memory_space=pltpu.SMEM)
     vmem = pl.BlockSpec(memory_space=pltpu.VMEM)
@@ -173,7 +183,7 @@
         compiler_params=pltpu.CompilerParams(vmem_limit_bytes=40 * 2**20),
         cost_estimate=pl.CostEstimate(flops=flops, bytes_accessed=20 * 2**20, transcendentals=0),
         name="triple_products",
-    )(columns, slots, aggregate, tile, prolong, blocks)
+    )(columns.T, slots.T, aggregate, tile, turned, blocks)
 
 
 def scatter_kernel(x_ref, out_ref, ybuf, zsend, zbuf, own, ysend_sem, yrecv_sem, zsend_sem, zrecv_sem):
@@ -286,7 +296,8 @@
 
 def shards(n_row, blocks, prolong, columns, aggregate, slots):
     tile = gather_rows(prolong, n_row)
-    packed = products(tile, prolong, blocks, columns, aggregate, slots)
+    turned = jnp.swapaxes(prolong, 1, 2)
+    packed = products(tile, turned, blocks, columns, aggregate, slots)
     result = scatter_cols(packed)
     return result.reshape(KC, CR_SLAB, 288).transpose(1, 0, 2)
 

time: 87.9 us -> 150 us (1.71)
  Pallas kernels: 84 us -> 147 us
    pallas_call x1, Pallas kernels: 38.3 us -> 101 us  [products(): pl.pallas_call(product_kernel, grid=(rows // ROWS_STEP,), out_shape=jax.S...]
    unnamed x9 -> x10, local copies, waits for them, and re-layouts: 3.52 us -> 3.29 us
where the time goes in v3:
time: 150 us
  Pallas kernels  147 us (98%)
  local copies, waits for them, and re-layouts  3.29 us (2%)
    pallas_call x1, Pallas kernels, products(): pl.pallas_call(product_kernel, grid=(rows // ROWS_STEP,), out_shape=jax.S...  101 us
    pallas_call x1, Pallas kernels, scatter_cols(): pl.pallas_call(scatter_kernel, out_shape=jax.ShapeDtypeStruct((KC * CR_SL...  33.8 us
    pallas_call x1, Pallas kernels, gather_rows(): pl.pallas_call(gather_kernel, out_shape=jax.ShapeDtypeStruct((n_row * row...  11.9 us
    unnamed x10, local copies, waits for them, and re-layouts  3.29 us

profile of v3, /device:TPU:0, one launch (start us, length us, event | category | flops | bytes accessed | tf_op | source)
XLA Modules:
  0.0 150.0 jit_solution(4448340058152505009)
XLA Ops:
  0.0 0.0 copy-start.2
  0.0 0.0 copy-start.3
  0.0 0.0 copy-start.1
  0.0 1.4 copy.6
  1.4 0.0 copy-start
  1.4 1.1 copy-done
  2.5 11.9 %gather_prolong.1.tile_ref = bf16[192,48,128]{2,1,0:T(8,128)(2,1)S(1)} custom-call(bf16[48,48,48]{2,1,0:T(8,128)(2,1)S(1)} %copy-done), custom_call_target="tpu_custom_call" | custom-call | tf_op jit(solution)/shard_map/gather_prolong/pallas_call | solution.py:88
  14.4 0.0 copy-done.2
  14.4 0.0 copy-done.3
  14.4 0.0 copy-done.1
  14.4 100.9 %triple_products.1.x_ref = bf16[8,112,1152]{2,1,0:T(8,128)(2,1)S(1)} custom-call(s32[27,48]{1,0:T(8,128)S(1)} %bitcast.8, s32[27,48]{1,0:T(8,128)S(1)} %bitcast.9, s32[48]{0:T(128)S(1)} %copy-done.3, bf16[192,48,128]{2,1,0:T(8,128)(2,1)S(1)} %gather_prolong.1.tile_ref, bf16[48,48,48]{2,1,0:T(8,128)(2,1)S(1)} %bitcast.7, bf16[48,27,48,48]{3,2,1,0:T(8,128)(2,1)} %blk_ref.1), custom_call_target="tpu_custom_call" | custom-call | flops 573308928 | bytes 20971520 | tf_op jit(solution)/shard_map/triple_products/pallas_call | solution.py:169
  115.3 33.8 %scatter_cols.1 = f32[432,288]{1,0:T(8,128)S(1)} custom-call(bf16[8,112,1152]{2,1,0:T(8,128)(2,1)S(1)} %triple_products.1.x_ref), custom_call_target="tpu_custom_call" | custom-call | tf_op jit(solution)/shard_map/scatter_cols/pallas_call | solution.py:275
  149.2 0.8 copy.8
Async XLA Ops:
  0.0 14.4 %copy-start.2 = (s32[48,27]{0,1:T(8,128)S(1)}, s32[48,27]{0,1:T(8,128)}, u32[]{:S(2)}) copy-start(s32[48,27]{0,1:T(8,128)} %param.9) | copy-start | bytes 15556
  0.0 14.4 %copy-start.3 = (s32[48]{0:T(128)S(1)}, s32[48]{0:T(128)}, u32[]{:S(2)}) copy-start(s32[48]{0:T(128)} %agg_ref.1) | copy-start | bytes 580
  0.0 14.4 %copy-start.1 = (s32[48,27]{0,1:T(8,128)S(1)}, s32[48,27]{0,1:T(8,128)}, u32[]{:S(2)}) copy-start(s32[48,27]{0,1:T(8,128)} %param.7) | copy-start | bytes 15556
  1.4 1.1 copy-start

commit v4 on v1

--- a/solution.py
+++ b/solution.py
@@ -14,6 +14,7 @@
 GROUPS = 4
 GROUP = 112
 ROWS_STEP = 4
+PARTS = 3
 HALVES = ((0, 64), (64, 48))
 
 
@@ -50,36 +51,45 @@
     packed[0] = both.astype(jnp.bfloat16)
     pl.semaphore_wait(barrier, 2)
 
-    def send(source, dest, peer):
+    step = half * width // PARTS
+    blocks = half // PARTS
+
+    def send(source, dest, part, peer):
         copy = pltpu.make_async_remote_copy(
-            src_ref=packed.at[source],
-            dst_ref=packed.at[dest],
-            send_sem=send_sem.at[dest],
-            recv_sem=recv_sem.at[dest],
+            src_ref=packed.at[source, pl.ds(part * step, step)],
+            dst_ref=packed.at[dest, pl.ds(part * step, step)],
+            send_sem=send_sem.at[dest, part],
+            recv_sem=recv_sem.at[dest, part],
             device_id={"row": peer},
             device_id_type=MESH,
         )
         copy.start()
         return copy
 
-    def unpack(slot, owner):
-        value = packed[slot]
-        out_ref[pl.ds(owner * rows, half)] = move(value, placement(LANES, 0, 0)).reshape(half, width, LANES)
-        out_ref[pl.ds(owner * rows + half, half)] = move(value, placement(LANES, 48, 0)).reshape(half, width, LANES)
-
-    far = send(0, 2, across)
-    near = send(0, 1, other)
-    unpack(0, me)
-    near.wait_recv()
-    unpack(1, other)
-    far.wait_recv()
-    relay = send(2, 3, other)
-    unpack(2, across)
-    relay.wait_recv()
-    unpack(3, diagonal)
-    far.wait_send()
-    near.wait_send()
-    relay.wait_send()
+    def unpack(slot, part, owner):
+        value = packed[slot, pl.ds(part * step, step), :]
+        for side in range(2):
+            at = owner * rows + half * side + part * blocks
+            piece = move(value, placement(LANES, 48 * side, 0))
+            out_ref[pl.ds(at, blocks)] = piece.reshape(blocks, width, LANES)
+
+    far = [send(0, 2, part, across) for part in range(PARTS)]
+    near = [send(0, 1, part, other) for part in range(PARTS)]
+    for part in range(PARTS):
+        unpack(0, part, me)
+    for part in range(PARTS):
+        near[part].wait_recv()
+        unpack(1, part, other)
+    relay = []
+    for part in range(PARTS):
+        far[part].wait_recv()
+        relay.append(send(2, 3, part, other))
+        unpack(2, part, across)
+    for part in range(PARTS):
+        relay[part].wait_recv()
+        unpack(3, part, diagonal)
+    for copy in far + near + relay:
+        copy.wait_send()
 
 
 def gather_rows(prolong, n_row):
@@ -91,8 +101,8 @@
         out_specs=pl.BlockSpec(memory_space=pltpu.VMEM),
         scratch_shapes=[
             pltpu.VMEM((4, rows // 2 * width, LANES), jnp.bfloat16),
-            pltpu.SemaphoreType.DMA((4,)),
-            pltpu.SemaphoreType.DMA((4,)),
+            pltpu.SemaphoreType.DMA((4, PARTS)),
+            pltpu.SemaphoreType.DMA((4, PARTS)),
         ],
         compiler_params=pltpu.CompilerParams(
             collective_id=0, has_side_effects=True, vmem_limit_bytes=24 * 2**20
@@ -101,7 +111,7 @@
     )(prolong)
 
 
-def product_kernel(col_ref, slot_ref, agg_ref, tile_ref, own_ref, blk_ref, out_ref, acc):
+def product_kernel(col_ref, slot_ref, agg_ref, tile_ref, own_ref, blk_ref, out_ref, acc, product, term, turned):
     step = pl.program_id(0)
     width = own_ref.shape[1]
     neighbours = blk_ref.shape[1]
@@ -112,18 +122,38 @@
         def _(at):
             acc[pl.ds(at * 384, 384), :] = jnp.zeros((384, LANES), jnp.float32)
 
+        product[...] = jnp.zeros_like(product)
+        term[...] = jnp.zeros_like(term)
+        turned[...] = jnp.zeros_like(turned)
+
+    last = own_ref.shape[0] - 1
+
+    def add_term(i, k):
+        base = pl.multiple_of((slot_ref[i, k] * CR_SLAB + agg_ref[i]) * width, width)
+        acc[pl.ds(base, width), :] += term[k]
+
+    def second(k):
+        term[k] = jnp.dot(turned[...], product[k], preferred_element_type=jnp.float32)
+
     @pl.loop(0, ROWS_STEP)
     def _(r):
         i = step * ROWS_STEP + r
-        turned = own_ref[i].astype(jnp.float32).T.astype(jnp.bfloat16)
-        aggregate = agg_ref[i]
+        before = jnp.maximum(i - 2, 0)
         for k in range(neighbours):
-            product = jnp.dot(
+            add_term(before, k)
+            second(k)
+            product[k] = jnp.dot(
                 blk_ref[r, k], tile_ref[col_ref[i, k]], preferred_element_type=jnp.float32
             ).astype(jnp.bfloat16)
-            term = jnp.dot(turned, product, preferred_element_type=jnp.float32)
-            base = pl.multiple_of((slot_ref[i, k] * CR_SLAB + aggregate) * width, width)
-            acc[pl.ds(base, width), :] += term
+        turned[...] = own_ref[i].astype(jnp.float32).T.astype(jnp.bfloat16)
+
+    @pl.when(step == pl.num_programs(0) - 1)
+    def _():
+        for k in range(neighbours):
+            add_term(last - 1, k)
+            second(k)
+        for k in range(neighbours):
+            add_term(last, k)
 
     @pl.when(step == pl.num_programs(0) - 1)
     def _():
@@ -169,7 +199,12 @@
             pl.BlockSpec((ROWS_STEP, neighbours, width, width), lambda g: (g, 0, 0, 0)),
         ],
         out_specs=vmem,
-        scratch_shapes=[pltpu.VMEM((GROUPS * GROUP * width, LANES), jnp.float32)],
+        scratch_shapes=[
+            pltpu.VMEM((GROUPS * GROUP * width, LANES), jnp.float32),
+            pltpu.VMEM((neighbours, width, LANES), jnp.bfloat16),
+            pltpu.VMEM((neighbours, width, LANES), jnp.float32),
+            pltpu.VMEM((width, width), jnp.bfloat16),
+        ],
         compiler_params=pltpu.CompilerParams(vmem_limit_bytes=40 * 2**20),
         cost_estimate=pl.CostEstimate(flops=flops, bytes_accessed=20 * 2**20, transcendentals=0),
         name="triple_products",

time: 87.9 us -> 83.4 us (0.949)
  Pallas kernels: 84 us -> 79.6 us
    pallas_call x1, Pallas kernels: 38.3 us -> 34 us  [products(): pl.pallas_call(product_kernel, grid=(rows // ROWS_STEP,), out_shape=jax.S...]
where the time goes in v4:
time: 83.4 us; the launch traced here: 83.1 us
  Pallas kernels  79.6 us (95%)
  local copies, waits for them, and re-layouts  3.52 us (4%)
    pallas_call x1, Pallas kernels, products(): pl.pallas_call(product_kernel, grid=(rows // ROWS_STEP,), out_shape=jax.S...  34 us
    pallas_call x1, Pallas kernels, scatter_cols(): pl.pallas_call(scatter_kernel, out_shape=jax.ShapeDtypeStruct((KC * CR_SL...  33.8 us
    pallas_call x1, Pallas kernels, gather_rows(): pl.pallas_call(gather_kernel, out_shape=jax.ShapeDtypeStruct((n_row * row...  11.8 us
    unnamed x9, local copies, waits for them, and re-layouts  3.52 us

profile of v4, /device:TPU:0, one launch (start us, length us, event | category | flops | bytes accessed | tf_op | source)
XLA Modules:
  0.0 83.1 jit_solution(15249980816695422718)
XLA Ops:
  0.0 0.0 copy-start.2
  0.0 0.8 copy.6.col_ref
  0.8 0.8 copy.7.slot_ref
  1.6 0.0 copy-start
  1.6 1.1 %copy-done = bf16[48,48,48]{2,1,0:T(8,128)(2,1)S(1)} copy-done((bf16[48,48,48]{2,1,0:T(8,128)(2,1)S(1)}, bf16[48,48,48]{2,1,0:T(8,128)(2,1)}, u32[]{:S(2)}) %copy-start) | copy-done | bytes 221208
  2.7 0.0 copy-start.1
  2.7 11.8 %gather_prolong.1.tile_ref = bf16[192,48,128]{2,1,0:T(8,128)(2,1)S(1)} custom-call(bf16[48,48,48]{2,1,0:T(8,128)(2,1)S(1)} %copy-done), custom_call_target="tpu_custom_call" | custom-call | tf_op jit(solution)/shard_map/gather_prolong/pallas_call | solution.py:97
  14.5 0.0 copy-done.2
  14.5 0.0 copy-done.1
  14.5 34.0 %triple_products.1.x_ref = bf16[8,112,1152]{2,1,0:T(8,128)(2,1)S(1)} custom-call(s32[48,27]{1,0:T(8,128)S(1)} %copy.6.col_ref, s32[48,27]{1,0:T(8,128)S(1)} %copy.7.slot_ref, s32[48]{0:T(128)S(1)} %copy-done.2, bf16[192,48,128]{2,1,0:T(8,128)(2,1)S(1)} %gather_prolong.1.tile_ref, bf16[48,48,48]{2,1,0:T(8,128)(2,1)S(1)} %copy-done.1, ...), custom_call_target="tpu_custom_call" | custom-call | flops 573308928 | bytes 20971520 | tf_op jit(solution)/shard_map/triple_products/pallas_call | solution.py:189
  48.5 33.8 %scatter_cols.1 = f32[432,288]{1,0:T(8,128)S(1)} custom-call(bf16[8,112,1152]{2,1,0:T(8,128)(2,1)S(1)} %triple_products.1.x_ref), custom_call_target="tpu_custom_call" | custom-call | tf_op jit(solution)/shard_map/scatter_cols/pallas_call | solution.py:300
  82.3 0.8 %copy.9 = f32[16,27,288]{2,0,1:T(8,128)} copy(f32[16,27,288]{2,0,1:T(8,128)S(1)} %bitcast.3) | data formatting | bytes 995328
Async XLA Ops:
  0.0 14.5 %copy-start.2 = (s32[48]{0:T(128)S(1)}, s32[48]{0:T(128)}, u32[]{:S(2)}) copy-start(s32[48]{0:T(128)} %agg_ref.1) | copy-start | bytes 580
  1.6 1.1 %copy-start = (bf16[48,48,48]{2,1,0:T(8,128)(2,1)S(1)}, bf16[48,48,48]{2,1,0:T(8,128)(2,1)}, u32[]{:S(2)}) copy-start(bf16[48,48,48]{2,1,0:T(8,128)(2,1)} %own_ref.1) | copy-start | bytes 663556
  2.7 11.8 %copy-start.1 = (bf16[48,48,48]{2,1,0:T(8,128)(2,1)S(1)}, bf16[48,48,48]{2,1,0:T(8,128)(2,1)}, u32[]{:S(2)}) copy-start(bf16[48,48,48]{2,1,0:T(8,128)(2,1)} %own_ref.1) | copy-start | bytes 663556

commit v5 on v4

--- a/solution.py
+++ b/solution.py
@@ -15,6 +15,7 @@
 GROUP = 112
 ROWS_STEP = 4
 PARTS = 3
+CHUNK = 9
 HALVES = ((0, 64), (64, 48))
 
 
@@ -29,7 +30,7 @@
     return jnp.dot(value, matrix, preferred_element_type=jnp.float32).astype(jnp.bfloat16)
 
 
-def gather_kernel(p_ref, out_ref, packed, send_sem, recv_sem):
+def gather_kernel(p_ref, out_ref, turned, packed, send_sem, recv_sem):
     rows, width = p_ref.shape[0], p_ref.shape[1]
     half = rows // 2
     me = lax.axis_index("row")
@@ -42,8 +43,13 @@
     for peer in (other, across):
         pl.semaphore_signal(barrier, inc=1, device_id={"row": peer}, device_id_type=MESH)
 
-    low = p_ref[:half].reshape(half * width, width)
-    high = p_ref[half:].reshape(half * width, width)
+    @pl.loop(0, rows // 8)
+    def _(at):
+        for n in range(8):
+            turned[at * 8 + n] = p_ref[at * 8 + n].astype(jnp.float32).T.astype(jnp.bfloat16)
+
+    low = turned[:half].reshape(half * width, width)
+    high = turned[half:].reshape(half * width, width)
     first, second = placement(width, 0, 0), placement(width, 0, 48)
     both = jnp.dot(low, first, preferred_element_type=jnp.float32) + jnp.dot(
         high, second, preferred_element_type=jnp.float32
@@ -100,6 +106,7 @@
         in_specs=[pl.BlockSpec(memory_space=pltpu.VMEM)],
         out_specs=pl.BlockSpec(memory_space=pltpu.VMEM),
         scratch_shapes=[
+            pltpu.VMEM((rows, width, width), jnp.bfloat16),
             pltpu.VMEM((4, rows // 2 * width, LANES), jnp.bfloat16),
             pltpu.SemaphoreType.DMA((4, PARTS)),
             pltpu.SemaphoreType.DMA((4, PARTS)),
@@ -111,7 +118,11 @@
     )(prolong)
 
 
-def product_kernel(col_ref, slot_ref, agg_ref, tile_ref, own_ref, blk_ref, out_ref, acc, product, term, turned):
+def turned_dot(left, right):
+    return lax.dot_general(left, right, (((1,), (1,)), ((), ())), preferred_element_type=jnp.float32)
+
+
+def product_kernel(col_ref, slot_ref, agg_ref, tile_ref, own_ref, blk_ref, out_ref, acc, product, term, back):
     step = pl.program_id(0)
     width = own_ref.shape[1]
     neighbours = blk_ref.shape[1]
@@ -120,65 +131,70 @@
     def _():
         @pl.loop(0, acc.shape[0] // 384)
         def _(at):
-            acc[pl.ds(at * 384, 384), :] = jnp.zeros((384, LANES), jnp.float32)
+            acc[pl.ds(at * 384, 384), :] = jnp.zeros((384, width), jnp.float32)
 
         product[...] = jnp.zeros_like(product)
         term[...] = jnp.zeros_like(term)
-        turned[...] = jnp.zeros_like(turned)
 
     last = own_ref.shape[0] - 1
 
     def add_term(i, k):
-        base = pl.multiple_of((slot_ref[i, k] * CR_SLAB + agg_ref[i]) * width, width)
-        acc[pl.ds(base, width), :] += term[k]
-
-    def second(k):
-        term[k] = jnp.dot(turned[...], product[k], preferred_element_type=jnp.float32)
+        base = pl.multiple_of((slot_ref[k, i] * CR_SLAB + agg_ref[i]) * width, width)
+        acc[pl.ds(base, width), :] += term[pl.ds(k * width, width), :]
+
+    def second(i, first, count):
+        rows = pl.ds(first * width, count * width)
+        term[rows, :] = jnp.dot(product[rows, :], own_ref[i], preferred_element_type=jnp.float32)
 
     @pl.loop(0, ROWS_STEP)
     def _(r):
         i = step * ROWS_STEP + r
-        before = jnp.maximum(i - 2, 0)
-        for k in range(neighbours):
-            add_term(before, k)
-            second(k)
-            product[k] = jnp.dot(
-                blk_ref[r, k], tile_ref[col_ref[i, k]], preferred_element_type=jnp.float32
-            ).astype(jnp.bfloat16)
-        turned[...] = own_ref[i].astype(jnp.float32).T.astype(jnp.bfloat16)
+        before, earlier = jnp.maximum(i - 1, 0), jnp.maximum(i - 2, 0)
+        for first in range(0, neighbours, CHUNK):
+            for k in range(first, first + CHUNK):
+                add_term(earlier, k)
+            second(before, first, CHUNK)
+            for k in range(first, first + CHUNK):
+                value = turned_dot(tile_ref[col_ref[k, i], :, :width], blk_ref[r, k])
+                product[pl.ds(k * width, width), :] = value.astype(jnp.bfloat16)
 
     @pl.when(step == pl.num_programs(0) - 1)
     def _():
-        for k in range(neighbours):
-            add_term(last - 1, k)
-            second(k)
+        for first in range(0, neighbours, CHUNK):
+            for k in range(first, first + CHUNK):
+                add_term(last - 1, k)
+            second(last, first, CHUNK)
         for k in range(neighbours):
             add_term(last, k)
 
-    @pl.when(step == pl.num_programs(0) - 1)
-    def _():
         lane = lax.broadcasted_iota(jnp.int32, (16, LANES), 1)
-
-        @pl.loop(0, 8 * (GROUP // 16))
-        def _(at):
-            d, s = at // (GROUP // 16), at % (GROUP // 16)
-            sums = [None] * 9
-            for q in range(GROUPS):
-                for r in range(6):
-                    start = (GROUP * q + 16 * s) * width + 6 * d + r
-                    offset = (q * 6 + r) * 48
-                    j, shift = offset // LANES, offset % LANES
-                    value = acc[pl.ds(start, 16, stride=width), :]
-                    if shift:
-                        value = pltpu.roll(value, shift, 1)
-                    over = shift + 48 - LANES
-                    if over > 0:
-                        spill = jnp.where(lane < over, value, 0.0)
-                        value = jnp.where(lane < over, 0.0, value)
-                        sums[j + 1] = spill
-                    sums[j] = value if sums[j] is None else sums[j] + value
-            for j in range(9):
-                out_ref[d, pl.ds(pl.multiple_of(16 * s, 16), 16), j * LANES:(j + 1) * LANES] = sums[j].astype(jnp.bfloat16)
+        same = placement(width, 0, 0)[:, :width]
+
+        @pl.loop(0, GROUP // 16)
+        def _(s):
+            for t in range(16):
+                sums = [
+                    acc[pl.ds(pl.multiple_of((GROUP * q + 16 * s + t) * width, width), width), :].astype(jnp.bfloat16)
+                    for q in range(GROUPS)
+                ]
+                value = turned_dot(same, jnp.concatenate(sums, axis=0))
+                back[0, pl.ds(t * width, width), :] = value[:, :LANES]
+                back[1, pl.ds(t * width, width), :GROUPS * width - LANES] = value[:, LANES:]
+
+            rows = pl.ds(pl.multiple_of(16 * s, 16), 16)
+
+            @pl.loop(0, 8)
+            def _(d):
+                for pair in range(3):
+                    at = 6 * d + 2 * pair
+                    low, high, low_next, high_next = (
+                        back[j, pl.ds(at + r, 16, stride=width), :] for r in range(2) for j in range(2)
+                    )
+                    low_next, high_next = pltpu.roll(low_next, 64, 1), pltpu.roll(high_next, 64, 1)
+                    parts = (low, jnp.where(lane < 64, high, low_next), jnp.where(lane < 64, low_next, high_next))
+                    for j, part in enumerate(parts):
+                        begin = (3 * pair + j) * LANES
+                        out_ref[d, rows, begin:begin + LANES] = part.astype(jnp.bfloat16)
 
 
 def products(tile, prolong, blocks, columns, aggregate, slots):
@@ -200,15 +216,15 @@
         ],
         out_specs=vmem,
         scratch_shapes=[
-            pltpu.VMEM((GROUPS * GROUP * width, LANES), jnp.float32),
-            pltpu.VMEM((neighbours, width, LANES), jnp.bfloat16),
-            pltpu.VMEM((neighbours, width, LANES), jnp.float32),
-            pltpu.VMEM((width, width), jnp.bfloat16),
+            pltpu.VMEM((GROUPS * GROUP * width, width), jnp.float32),
+            pltpu.VMEM((neighbours * width, width), jnp.bfloat16),
+            pltpu.VMEM((neighbours * width, width), jnp.float32),
+            pltpu.VMEM((2, 16 * width, LANES), jnp.float32),
         ],
         compiler_params=pltpu.CompilerParams(vmem_limit_bytes=40 * 2**20),
         cost_estimate=pl.CostEstimate(flops=flops, bytes_accessed=20 * 2**20, transcendentals=0),
         name="triple_products",
-    )(columns, slots, aggregate, tile, prolong, blocks)
+    )(columns.T, slots.T, aggregate, tile, prolong, blocks)
 
 
 def scatter_kernel(x_ref, out_ref, ybuf, zsend, zbuf, own, ysend_sem, yrecv_sem, zsend_sem, zrecv_sem):
@@ -272,18 +288,23 @@
         total = own[rows, :]
         for s in range(3):
             total = total + zbuf[s, rows, :].astype(jnp.float32)
+        tiles = [total[:, j * LANES:(j + 1) * LANES] for j in range(9)]
         for q in range(groups):
-            j, shift = 288 * q // LANES, 288 * q % LANES
-            turned = [total[:, (j + m) * LANES:(j + m + 1) * LANES] for m in range(3)]
-            if shift:
-                turned = [pltpu.roll(piece, LANES - shift, 1) for piece in turned]
+            parts = [None] * 3
+            for r in range(6):
+                source, dest = 192 * r + 48 * q, 48 * r
+                shift = (dest - source) % LANES
+                for j in range(source // LANES, (source + 47) // LANES + 1):
+                    begin = max(source, LANES * j) - source + dest
+                    end = min(source + 48, LANES * (j + 1)) - source + dest
+                    piece = pltpu.roll(tiles[j], shift, 1) if shift else tiles[j]
+                    for m in range(begin // LANES, (end - 1) // LANES + 1):
+                        low = max(begin - LANES * m, 0)
+                        parts[m] = jnp.where(lane < low, parts[m], piece) if low else piece
             target = pl.ds(pl.multiple_of(GROUP * q + at * 16, 16), 16)
             for m in range(2):
-                piece = turned[m]
-                if shift:
-                    piece = jnp.where(lane < LANES - shift, piece, turned[m + 1])
-                out_ref[target, m * LANES:(m + 1) * LANES] = piece
-            out_ref[target, 256:288] = turned[2][:, :32]
+                out_ref[target, m * LANES:(m + 1) * LANES] = parts[m]
+            out_ref[target, 256:288] = parts[2][:, :32]
 
     @pl.loop(0, 6)
     def _(at):

time: 83.4 us -> 84.6 us (1.014)
  Pallas kernels: 79.6 us -> 82.4 us
  local copies, waits for them, and re-layouts: 3.52 us -> 1.93 us
    pallas_call x1, Pallas kernels: 34 us -> 36.5 us  [products(): pl.pallas_call(product_kernel, grid=(rows // ROWS_STEP,), out_shape=jax.S...]
    unnamed x9 -> x11, local copies, waits for them, and re-layouts: 3.52 us -> 1.93 us
where the time goes in v5:
time: 84.6 us; the launch traced here: 84.4 us
  Pallas kernels  82.4 us (97%)
  local copies, waits for them, and re-layouts  1.93 us (2%)
    pallas_call x1, Pallas kernels, products(): pl.pallas_call(product_kernel, grid=(rows // ROWS_STEP,), out_shape=jax.S...  36.5 us
    pallas_call x1, Pallas kernels, scatter_cols(): pl.pallas_call(scatter_kernel, out_shape=jax.ShapeDtypeStruct((KC * CR_SL...  33.9 us
    pallas_call x1, Pallas kernels, gather_rows(): pl.pallas_call(gather_kernel, out_shape=jax.ShapeDtypeStruct((n_row * row...  12.1 us
    unnamed x11, local copies, waits for them, and re-layouts  1.93 us

profile of v5, /device:TPU:0, one launch (start us, length us, event | category | flops | bytes accessed | tf_op | source)
XLA Modules:
  0.0 84.4 jit_solution(5438152000382610567)
XLA Ops:
  0.0 0.0 copy-start.4
  0.0 0.0 copy-start
  0.0 1.1 %copy-done = bf16[48,48,48]{2,1,0:T(8,128)(2,1)S(1)} copy-done((bf16[48,48,48]{2,1,0:T(8,128)(2,1)S(1)}, bf16[48,48,48]{2,1,0:T(8,128)(2,1)}, u32[]{:S(2)}) %copy-start) | copy-done | bytes 221208
  1.1 0.0 copy-start.1
  1.1 0.0 copy-start.2
  1.1 0.0 copy-start.3
  1.1 12.1 %gather_prolong.1.tile_ref = bf16[192,48,128]{2,1,0:T(8,128)(2,1)S(1)} custom-call(bf16[48,48,48]{2,1,0:T(8,128)(2,1)S(1)} %copy-done), custom_call_target="tpu_custom_call" | custom-call | tf_op jit(solution)/shard_map/gather_prolong/pallas_call | solution.py:103
  13.2 0.0 copy-done.4
  13.2 0.0 copy-done.1
  13.2 0.0 copy-done.2
  13.2 0.0 copy-done.3
  13.2 36.5 %triple_products.1.x_ref = bf16[8,112,1152]{2,1,0:T(8,128)(2,1)S(1)} custom-call(s32[27,48]{1,0:T(8,128)S(1)} %bitcast.6, s32[27,48]{1,0:T(8,128)S(1)} %bitcast.7, s32[48]{0:T(128)S(1)} %copy-done.4, bf16[192,48,128]{2,1,0:T(8,128)(2,1)S(1)} %gather_prolong.1.tile_ref, bf16[48,48,48]{2,1,0:T(8,128)(2,1)S(1)} %copy-done.1, bf16[48,27,48,48]{3,2,1,0:T(8,128)(2,1)} %blk_ref.1), custom_call_target="tpu_custom_call" | custom-call | flops 573308928 | bytes 20971520 | tf_op jit(solution)/shard_map/triple_products/pallas_call | solution.py:205
  49.7 33.9 %scatter_cols.1 = f32[432,288]{1,0:T(8,128)S(1)} custom-call(bf16[8,112,1152]{2,1,0:T(8,128)(2,1)S(1)} %triple_products.1.x_ref), custom_call_target="tpu_custom_call" | custom-call | tf_op jit(solution)/shard_map/scatter_cols/pallas_call | solution.py:321
  83.6 0.8 copy.7
Async XLA Ops:
  0.0 13.2 %copy-start.4 = (s32[48]{0:T(128)S(1)}, s32[48]{0:T(128)}, u32[]{:S(2)}) copy-start(s32[48]{0:T(128)} %agg_ref.1) | copy-start | bytes 580
  0.0 1.1 %copy-start = (bf16[48,48,48]{2,1,0:T(8,128)(2,1)S(1)}, bf16[48,48,48]{2,1,0:T(8,128)(2,1)}, u32[]{:S(2)}) copy-start(bf16[48,48,48]{2,1,0:T(8,128)(2,1)} %own_ref.1) | copy-start | bytes 663556
  1.1 12.1 %copy-start.1 = (bf16[48,48,48]{2,1,0:T(8,128)(2,1)S(1)}, bf16[48,48,48]{2,1,0:T(8,128)(2,1)}, u32[]{:S(2)}) copy-start(bf16[48,48,48]{2,1,0:T(8,128)(2,1)} %own_ref.1) | copy-start | bytes 663556
  1.1 12.1 %copy-start.2 = (s32[48,27]{0,1:T(8,128)S(1)}, s32[48,27]{0,1:T(8,128)}, u32[]{:S(2)}) copy-start(s32[48,27]{0,1:T(8,128)} %param.7) | copy-start | bytes 15556
  1.1 12.2 %copy-start.3 = (s32[48,27]{0,1:T(8,128)S(1)}, s32[48,27]{0,1:T(8,128)}, u32[]{:S(2)}) copy-start(s32[48,27]{0,1:T(8,128)} %param.9) | copy-start | bytes 15556

commit v6 on v4

--- a/solution.py
+++ b/solution.py
@@ -15,7 +15,7 @@
 GROUP = 112
 ROWS_STEP = 4
 PARTS = 3
-HALVES = ((0, 64), (64, 48))
+HALVES = ((0, 32), (32, 32), (64, 32), (96, 16))
 
 
 def placement(rows, source, dest):
@@ -128,9 +128,18 @@
 
     last = own_ref.shape[0] - 1
 
-    def add_term(i, k):
-        base = pl.multiple_of((slot_ref[i, k] * CR_SLAB + agg_ref[i]) * width, width)
-        acc[pl.ds(base, width), :] += term[k]
+    def add_terms(i, first):
+        group = range(first, first + 3)
+        slot = [slot_ref[k, i] for k in group]
+        rows = [pl.ds(pl.multiple_of((n * CR_SLAB + agg_ref[i]) * width, width), width) for n in slot]
+        old = [acc[at, :] for at in rows]
+        terms = [term[k] for k in group]
+        sums = list(terms)
+        for later in range(1, 3):
+            for earlier in range(later):
+                sums[later] += jnp.where(slot[earlier] == slot[later], terms[earlier], 0.0)
+        for at in range(3):
+            acc[rows[at], :] = old[at] + sums[at]
 
     def second(k):
         term[k] = jnp.dot(turned[...], product[k], preferred_element_type=jnp.float32)
@@ -139,21 +148,24 @@
     def _(r):
         i = step * ROWS_STEP + r
         before = jnp.maximum(i - 2, 0)
-        for k in range(neighbours):
-            add_term(before, k)
-            second(k)
-            product[k] = jnp.dot(
-                blk_ref[r, k], tile_ref[col_ref[i, k]], preferred_element_type=jnp.float32
-            ).astype(jnp.bfloat16)
+        for first in range(0, neighbours, 3):
+            add_terms(before, first)
+            for k in range(first, first + 3):
+                second(k)
+            for k in range(first, first + 3):
+                product[k] = jnp.dot(
+                    blk_ref[r, k], tile_ref[col_ref[k, i]], preferred_element_type=jnp.float32
+                ).astype(jnp.bfloat16)
         turned[...] = own_ref[i].astype(jnp.float32).T.astype(jnp.bfloat16)
 
     @pl.when(step == pl.num_programs(0) - 1)
     def _():
-        for k in range(neighbours):
-            add_term(last - 1, k)
-            second(k)
-        for k in range(neighbours):
-            add_term(last, k)
+        for first in range(0, neighbours, 3):
+            add_terms(last - 1, first)
+            for k in range(first, first + 3):
+                second(k)
+        for first in range(0, neighbours, 3):
+            add_terms(last, first)
 
     @pl.when(step == pl.num_programs(0) - 1)
     def _():
@@ -208,7 +220,7 @@
         compiler_params=pltpu.CompilerParams(vmem_limit_bytes=40 * 2**20),
         cost_estimate=pl.CostEstimate(flops=flops, bytes_accessed=20 * 2**20, transcendentals=0),
         name="triple_products",
-    )(columns, slots, aggregate, tile, prolong, blocks)
+    )(columns.T, slots.T, aggregate, tile, prolong, blocks)
 
 
 def scatter_kernel(x_ref, out_ref, ybuf, zsend, zbuf, own, ysend_sem, yrecv_sem, zsend_sem, zrecv_sem):
@@ -262,13 +274,10 @@
                 copy.start()
                 zcopies[s, h] = copy
 
-    for copy in zcopies.values():
-        copy.wait_recv()
-
     lane = lax.broadcasted_iota(jnp.int32, (16, LANES), 1)
 
     def unpack(at, groups):
-        rows = pl.ds(pl.multiple_of(at * 16, 16), 16)
+        rows = pl.ds(at * 16, 16)
         total = own[rows, :]
         for s in range(3):
             total = total + zbuf[s, rows, :].astype(jnp.float32)
@@ -277,7 +286,7 @@
             turned = [total[:, (j + m) * LANES:(j + m + 1) * LANES] for m in range(3)]
             if shift:
                 turned = [pltpu.roll(piece, LANES - shift, 1) for piece in turned]
-            target = pl.ds(pl.multiple_of(GROUP * q + at * 16, 16), 16)
+            target = pl.ds(GROUP * q + at * 16, 16)
             for m in range(2):
                 piece = turned[m]
                 if shift:
@@ -285,11 +294,11 @@
                 out_ref[target, m * LANES:(m + 1) * LANES] = piece
             out_ref[target, 256:288] = turned[2][:, :32]
 
-    @pl.loop(0, 6)
-    def _(at):
-        unpack(at, 4)
-
-    unpack(6, 3)
+    for h, (begin, size) in enumerate(HALVES):
+        for s in range(3):
+            zcopies[s, h].wait_recv()
+        for at in range(begin // 16, (begin + size) // 16):
+            unpack(at, 4 if at < 6 else 3)
 
     for copy in list(ycopies.values()) + list(zcopies.values()):
         copy.wait_send()

time: 83.4 us -> 79.4 us (0.952)
  Pallas kernels: 79.6 us -> 77.3 us
  local copies, waits for them, and re-layouts: 3.52 us -> 1.93 us
    pallas_call x1, Pallas kernels: 33.8 us -> 31.9 us  [scatter_cols(): pl.pallas_call(scatter_kernel, out_shape=jax.ShapeDtypeStruct((KC * CR_SL...]
    unnamed x9 -> x11, local copies, waits for them, and re-layouts: 3.52 us -> 1.93 us
where the time goes in v6:
time: 79.4 us; the launch traced here: 79.3 us
  Pallas kernels  77.3 us (97%)
  local copies, waits for them, and re-layouts  1.93 us (2%)
    pallas_call x1, Pallas kernels, products(): pl.pallas_call(product_kernel, grid=(rows // ROWS_STEP,), out_shape=jax.S...  33.6 us
    pallas_call x1, Pallas kernels, scatter_cols(): pl.pallas_call(scatter_kernel, out_shape=jax.ShapeDtypeStruct((KC * CR_SL...  31.9 us
    pallas_call x1, Pallas kernels, gather_rows(): pl.pallas_call(gather_kernel, out_shape=jax.ShapeDtypeStruct((n_row * row...  11.8 us
    unnamed x11, local copies, waits for them, and re-layouts  1.93 us

profile of v6, /device:TPU:0, one launch (start us, length us, event | category | flops | bytes accessed | tf_op | source)
XLA Modules:
  0.0 79.3 jit_solution(14684289389549183541)
XLA Ops:
  0.0 0.0 copy-start.4
  0.0 0.0 copy-start
  0.0 1.1 %copy-done = bf16[48,48,48]{2,1,0:T(8,128)(2,1)S(1)} copy-done((bf16[48,48,48]{2,1,0:T(8,128)(2,1)S(1)}, bf16[48,48,48]{2,1,0:T(8,128)(2,1)}, u32[]{:S(2)}) %copy-start) | copy-done | bytes 221208
  1.1 0.0 copy-start.1
  1.1 0.0 copy-start.2
  1.1 0.0 copy-start.3
  1.1 11.8 %gather_prolong.1.tile_ref = bf16[192,48,128]{2,1,0:T(8,128)(2,1)S(1)} custom-call(bf16[48,48,48]{2,1,0:T(8,128)(2,1)S(1)} %copy-done), custom_call_target="tpu_custom_call" | custom-call | tf_op jit(solution)/shard_map/gather_prolong/pallas_call | solution.py:97
  12.9 0.0 copy-done.4
  12.9 0.0 copy-done.1
  12.9 0.0 copy-done.2
  12.9 0.0 copy-done.3
  12.9 33.6 %triple_products.1.x_ref = bf16[8,112,1152]{2,1,0:T(8,128)(2,1)S(1)} custom-call(s32[27,48]{1,0:T(8,128)S(1)} %bitcast.6, s32[27,48]{1,0:T(8,128)S(1)} %bitcast.7, s32[48]{0:T(128)S(1)} %copy-done.4, bf16[192,48,128]{2,1,0:T(8,128)(2,1)S(1)} %gather_prolong.1.tile_ref, bf16[48,48,48]{2,1,0:T(8,128)(2,1)S(1)} %copy-done.1, bf16[48,27,48,48]{3,2,1,0:T(8,128)(2,1)} %blk_ref.1), custom_call_target="tpu_custom_call" | custom-call | flops 573308928 | bytes 20971520 | tf_op jit(solution)/shard_map/triple_products/pallas_call | solution.py:201
  46.6 31.9 %scatter_cols.1 = f32[432,288]{1,0:T(8,128)S(1)} custom-call(bf16[8,112,1152]{2,1,0:T(8,128)(2,1)S(1)} %triple_products.1.x_ref), custom_call_target="tpu_custom_call" | custom-call | tf_op jit(solution)/shard_map/scatter_cols/pallas_call | solution.py:309
  78.4 0.8 %copy.7 = f32[16,27,288]{2,0,1:T(8,128)} copy(f32[16,27,288]{2,0,1:T(8,128)S(1)} %bitcast.5) | data formatting | bytes 995328
Async XLA Ops:
  0.0 12.9 %copy-start.4 = (s32[48]{0:T(128)S(1)}, s32[48]{0:T(128)}, u32[]{:S(2)}) copy-start(s32[48]{0:T(128)} %agg_ref.1) | copy-start | bytes 580
  0.0 1.1 %copy-start = (bf16[48,48,48]{2,1,0:T(8,128)(2,1)S(1)}, bf16[48,48,48]{2,1,0:T(8,128)(2,1)}, u32[]{:S(2)}) copy-start(bf16[48,48,48]{2,1,0:T(8,128)(2,1)} %own_ref.1) | copy-start | bytes 663556
  1.1 11.8 %copy-start.1 = (bf16[48,48,48]{2,1,0:T(8,128)(2,1)S(1)}, bf16[48,48,48]{2,1,0:T(8,128)(2,1)}, u32[]{:S(2)}) copy-start(bf16[48,48,48]{2,1,0:T(8,128)(2,1)} %own_ref.1) | copy-start | bytes 663556
  1.1 11.8 %copy-start.2 = (s32[48,27]{0,1:T(8,128)S(1)}, s32[48,27]{0,1:T(8,128)}, u32[]{:S(2)}) copy-start(s32[48,27]{0,1:T(8,128)} %param.7) | copy-start | bytes 15556
  1.1 11.8 %copy-start.3 = (s32[48,27]{0,1:T(8,128)S(1)}, s32[48,27]{0,1:T(8,128)}, u32[]{:S(2)}) copy-start(s32[48,27]{0,1:T(8,128)} %param.9) | copy-start | bytes 15556

commit v7 on v6

--- a/solution.py
+++ b/solution.py
@@ -111,7 +111,7 @@
     )(prolong)
 
 
-def product_kernel(col_ref, slot_ref, agg_ref, tile_ref, own_ref, blk_ref, out_ref, acc, product, term, turned):
+def product_kernel(col_ref, slot_ref, agg_ref, tile_ref, own_ref, blk_ref, acc, product, term, turned):
     step = pl.program_id(0)
     width = own_ref.shape[1]
     neighbours = blk_ref.shape[1]
@@ -167,31 +167,6 @@
         for first in range(0, neighbours, 3):
             add_terms(last, first)
 
-    @pl.when(step == pl.num_programs(0) - 1)
-    def _():
-        lane = lax.broadcasted_iota(jnp.int32, (16, LANES), 1)
-
-        @pl.loop(0, 8 * (GROUP // 16))
-        def _(at):
-            d, s = at // (GROUP // 16), at % (GROUP // 16)
-            sums = [None] * 9
-            for q in range(GROUPS):
-                for r in range(6):
-                    start = (GROUP * q + 16 * s) * width + 6 * d + r
-                    offset = (q * 6 + r) * 48
-                    j, shift = offset // LANES, offset % LANES
-                    value = acc[pl.ds(start, 16, stride=width), :]
-                    if shift:
-                        value = pltpu.roll(value, shift, 1)
-                    over = shift + 48 - LANES
-                    if over > 0:
-                        spill = jnp.where(lane < over, value, 0.0)
-                        value = jnp.where(lane < over, 0.0, value)
-                        sums[j + 1] = spill
-                    sums[j] = value if sums[j] is None else sums[j] + value
-            for j in range(9):
-                out_ref[d, pl.ds(pl.multiple_of(16 * s, 16), 16), j * LANES:(j + 1) * LANES] = sums[j].astype(jnp.bfloat16)
-
 
 def products(tile, prolong, blocks, columns, aggregate, slots):
     rows, neighbours, width = blocks.shape[0], blocks.shape[1], blocks.shape[2]
@@ -201,7 +176,7 @@
     return pl.pallas_call(
         product_kernel,
         grid=(rows // ROWS_STEP,),
-        out_shape=jax.ShapeDtypeStruct((8, GROUP, 9 * LANES), jnp.bfloat16),
+        out_shape=jax.ShapeDtypeStruct((GROUPS * GROUP * width, LANES), jnp.float32),
         in_specs=[
             smem,
             smem,
@@ -212,7 +187,6 @@
         ],
         out_specs=vmem,
         scratch_shapes=[
-            pltpu.VMEM((GROUPS * GROUP * width, LANES), jnp.float32),
             pltpu.VMEM((neighbours, width, LANES), jnp.bfloat16),
             pltpu.VMEM((neighbours, width, LANES), jnp.float32),
             pltpu.VMEM((width, width), jnp.bfloat16),
@@ -223,7 +197,24 @@
     )(columns.T, slots.T, aggregate, tile, prolong, blocks)
 
 
-def scatter_kernel(x_ref, out_ref, ybuf, zsend, zbuf, own, ysend_sem, yrecv_sem, zsend_sem, zrecv_sem):
+def pack_rows(acc, d, at):
+    lane = lax.broadcasted_iota(jnp.int32, (16, LANES), 1)
+    sums = [None] * 9
+    for q in range(GROUPS):
+        for r in range(6):
+            start = (GROUP * q + 16 * at) * 48 + 6 * d + r
+            offset = (q * 6 + r) * 48
+            j, shift = offset // LANES, offset % LANES
+            value = acc[pl.ds(start, 16, stride=48), :]
+            if shift:
+                value = pltpu.roll(value, shift, 1)
+            sums[j] = jnp.where(lane < shift, sums[j], value) if shift else value
+            if shift + 48 > LANES:
+                sums[j + 1] = value
+    return sums
+
+
+def scatter_kernel(acc, out_ref, ysend, ybuf, zsend, zbuf, own, ysend_sem, yrecv_sem, zsend_sem, zrecv_sem):
     me = lax.axis_index("col")
     y, z = me % 2, me // 2
     partner = z * 2 + 1 - y
@@ -233,13 +224,21 @@
     barrier = pltpu.get_barrier_semaphore()
     for peer in [partner] + [t * 2 + y for t in targets[:3]]:
         pl.semaphore_signal(barrier, inc=1, device_id={"col": peer}, device_id_type=MESH)
-    pl.semaphore_wait(barrier, 4)
 
     ycopies, zcopies = {}, {}
     for s in range(4):
         for h, (begin, size) in enumerate(HALVES):
+
+            @pl.loop(begin // 16, (begin + size) // 16)
+            def _(at):
+                rows = pl.ds(pl.multiple_of(at * 16, 16), 16)
+                for j, part in enumerate(pack_rows(acc, targets[s] * 2 + 1 - y, at)):
+                    ysend[s, rows, j * LANES:(j + 1) * LANES] = part.astype(jnp.bfloat16)
+
+            if s == 0 and h == 0:
+                pl.semaphore_wait(barrier, 4)
             copy = pltpu.make_async_remote_copy(
-                src_ref=x_ref.at[targets[s] * 2 + 1 - y, pl.ds(begin, size)],
+                src_ref=ysend.at[s, pl.ds(begin, size)],
                 dst_ref=ybuf.at[s, pl.ds(begin, size)],
                 send_sem=ysend_sem.at[s, h],
                 recv_sem=yrecv_sem.at[s, h],
@@ -256,11 +255,13 @@
             @pl.loop(begin // 16, (begin + size) // 16)
             def _(at):
                 rows = pl.ds(pl.multiple_of(at * 16, 16), 16)
-                total = x_ref[targets[s] * 2 + y, rows, :].astype(jnp.float32) + ybuf[s, rows, :].astype(jnp.float32)
-                if s < 3:
-                    zsend[s, rows, :] = total.astype(jnp.bfloat16)
-                else:
-                    own[rows, :] = total
+                for j, part in enumerate(pack_rows(acc, targets[s] * 2 + y, at)):
+                    lanes = slice(j * LANES, (j + 1) * LANES)
+                    total = part + ybuf[s, rows, lanes].astype(jnp.float32)
+                    if s < 3:
+                        zsend[s, rows, lanes] = total.astype(jnp.bfloat16)
+                    else:
+                        own[rows, lanes] = total
 
             if s < 3:
                 copy = pltpu.make_async_remote_copy(
@@ -313,6 +314,7 @@
         out_specs=pl.BlockSpec(memory_space=pltpu.VMEM),
         scratch_shapes=[
             pltpu.VMEM((4, GROUP, 9 * LANES), jnp.bfloat16),
+            pltpu.VMEM((4, GROUP, 9 * LANES), jnp.bfloat16),
             pltpu.VMEM((3, GROUP, 9 * LANES), jnp.bfloat16),
             pltpu.VMEM((3, GROUP, 9 * LANES), jnp.bfloat16),
             pltpu.VMEM((GROUP, 9 * LANES), jnp.float32),

time: 79.4 us -> 75.9 us (0.956)
  Pallas kernels: 77.3 us -> 70.4 us
  local copies, waits for them, and re-layouts: 1.93 us -> 5.05 us
    pallas_call x1, Pallas kernels: 33.6 us -> 26.6 us  [products(): pl.pallas_call(product_kernel, grid=(rows // ROWS_STEP,), out_shape=jax.S...]
    unnamed x11, local copies, waits for them, and re-layouts: 1.93 us -> 5.05 us
where the time goes in v7:
time: 75.9 us; the launch traced here: 75.5 us
  Pallas kernels  70.4 us (93%)
  local copies, waits for them, and re-layouts  5.05 us (7%)
    pallas_call x1, Pallas kernels, scatter_cols(): pl.pallas_call(scatter_kernel, out_shape=jax.ShapeDtypeStruct((KC * CR_SL...  32.1 us
    pallas_call x1, Pallas kernels, products(): pl.pallas_call(product_kernel, grid=(rows // ROWS_STEP,), out_shape=jax.S...  26.6 us
    pallas_call x1, Pallas kernels, gather_rows(): pl.pallas_call(gather_kernel, out_shape=jax.ShapeDtypeStruct((n_row * row...  11.8 us
    unnamed x11, local copies, waits for them, and re-layouts  5.05 us

profile of v7, /device:TPU:0, one launch (start us, length us, event | category | flops | bytes accessed | tf_op | source)
XLA Modules:
  0.0 75.5 jit_solution(3561430630866992691)
XLA Ops:
  0.0 0.0 copy-start
  0.0 1.1 %copy-done = bf16[48,48,48]{2,1,0:T(8,128)(2,1)S(1)} copy-done((bf16[48,48,48]{2,1,0:T(8,128)(2,1)S(1)}, bf16[48,48,48]{2,1,0:T(8,128)(2,1)}, u32[]{:S(2)}) %copy-start) | copy-done | bytes 221208
  1.1 11.8 %gather_prolong.1.tile_ref = bf16[192,48,128]{2,1,0:T(8,128)(2,1)S(1)} custom-call(bf16[48,48,48]{2,1,0:T(8,128)(2,1)S(1)} %copy-done), custom_call_target="tpu_custom_call" | custom-call | tf_op jit(solution)/shard_map/gather_prolong/pallas_call | solution.py:97
  12.9 0.0 copy-start.1
  12.9 1.1 %copy-done.1 = bf16[48,48,48]{2,1,0:T(8,128)(2,1)S(1)} copy-done((bf16[48,48,48]{2,1,0:T(8,128)(2,1)S(1)}, bf16[48,48,48]{2,1,0:T(8,128)(2,1)}, u32[]{:S(2)}) %copy-start.1) | copy-done | bytes 221208
  13.9 0.0 copy-start.2
  13.9 0.7 copy-done.2
  14.6 0.0 copy-start.3
  14.6 0.7 copy-done.3
  15.4 0.0 copy-start.4
  15.4 0.7 copy-done.4
  16.0 26.6 %triple_products.1.acc = f32[21504,128]{1,0:T(8,128)S(1)} custom-call(s32[27,48]{1,0:T(8,128)S(1)} %bitcast.6, s32[27,48]{1,0:T(8,128)S(1)} %bitcast.7, s32[48]{0:T(128)S(1)} %copy-done.4, bf16[192,48,128]{2,1,0:T(8,128)(2,1)S(1)} %gather_prolong.1.tile_ref, bf16[48,48,48]{2,1,0:T(8,128)(2,1)S(1)} %copy-done.1, bf16[48,27,48,48]{3,2,1,0:T(8,128)(2,1)} %blk_ref.1), custom_call_target="tpu_custom_call" | custom-call | flops 573308928 | bytes 20971520 | tf_op jit(solution)/shard_map/triple_products/pallas_call | solution.py:176
  42.6 32.1 %scatter_cols.1 = f32[432,288]{1,0:T(8,128)S(1)} custom-call(f32[21504,128]{1,0:T(8,128)S(1)} %triple_products.1.acc), custom_call_target="tpu_custom_call" | custom-call | tf_op jit(solution)/shard_map/scatter_cols/pallas_call | solution.py:310
  74.7 0.8 %copy.7 = f32[16,27,288]{2,0,1:T(8,128)} copy(f32[16,27,288]{2,0,1:T(8,128)S(1)} %bitcast.5) | data formatting | bytes 995328
Async XLA Ops:
  0.0 1.1 %copy-start = (bf16[48,48,48]{2,1,0:T(8,128)(2,1)S(1)}, bf16[48,48,48]{2,1,0:T(8,128)(2,1)}, u32[]{:S(2)}) copy-start(bf16[48,48,48]{2,1,0:T(8,128)(2,1)} %own_ref.1) | copy-start | bytes 663556
  12.9 1.1 %copy-start.1 = (bf16[48,48,48]{2,1,0:T(8,128)(2,1)S(1)}, bf16[48,48,48]{2,1,0:T(8,128)(2,1)}, u32[]{:S(2)}) copy-start(bf16[48,48,48]{2,1,0:T(8,128)(2,1)} %own_ref.1) | copy-start | bytes 663556
  13.9 0.7 copy-start.2
  14.6 0.7 copy-start.3
  15.4 0.7 copy-start.4

commit v8 on v7

--- a/solution.py
+++ b/solution.py
@@ -13,7 +13,7 @@
 LANES = 128
 GROUPS = 4
 GROUP = 112
-ROWS_STEP = 4
+ROWS_STEP = 8
 PARTS = 3
 HALVES = ((0, 32), (32, 32), (64, 32), (96, 16))
 

time: 75.9 us -> 76.1 us (level)
  no operation moved by 1% of the time
where the time goes in v8:
time: 76.1 us; the launch traced here: 75.7 us
  Pallas kernels  70.6 us (93%)
  local copies, waits for them, and re-layouts  5.05 us (7%)
    pallas_call x1, Pallas kernels, scatter_cols(): pl.pallas_call(scatter_kernel, out_shape=jax.ShapeDtypeStruct((KC * CR_SL...  32.1 us
    pallas_call x1, Pallas kernels, products(): pl.pallas_call(product_kernel, grid=(rows // ROWS_STEP,), out_shape=jax.S...  26.8 us
    pallas_call x1, Pallas kernels, gather_rows(): pl.pallas_call(gather_kernel, out_shape=jax.ShapeDtypeStruct((n_row * row...  11.8 us
    unnamed x11, local copies, waits for them, and re-layouts  5.05 us

profile of v8, /device:TPU:0, one launch (start us, length us, event | category | flops | bytes accessed | tf_op | source)
XLA Modules:
  0.0 75.7 jit_solution(12990697246442324199)
XLA Ops:
  0.0 0.0 copy-start
  0.0 1.1 %copy-done = bf16[48,48,48]{2,1,0:T(8,128)(2,1)S(1)} copy-done((bf16[48,48,48]{2,1,0:T(8,128)(2,1)S(1)}, bf16[48,48,48]{2,1,0:T(8,128)(2,1)}, u32[]{:S(2)}) %copy-start) | copy-done | bytes 221208
  1.1 11.8 %gather_prolong.1.tile_ref = bf16[192,48,128]{2,1,0:T(8,128)(2,1)S(1)} custom-call(bf16[48,48,48]{2,1,0:T(8,128)(2,1)S(1)} %copy-done), custom_call_target="tpu_custom_call" | custom-call | tf_op jit(solution)/shard_map/gather_prolong/pallas_call | solution.py:97
  12.9 0.0 copy-start.1
  12.9 1.1 %copy-done.1 = bf16[48,48,48]{2,1,0:T(8,128)(2,1)S(1)} copy-done((bf16[48,48,48]{2,1,0:T(8,128)(2,1)S(1)}, bf16[48,48,48]{2,1,0:T(8,128)(2,1)}, u32[]{:S(2)}) %copy-start.1) | copy-done | bytes 221208
  13.9 0.0 copy-start.2
  13.9 0.7 copy-done.2
  14.6 0.0 copy-start.3
  14.6 0.7 copy-done.3
  15.4 0.0 copy-start.4
  15.4 0.7 copy-done.4
  16.0 26.8 %triple_products.1.acc = f32[21504,128]{1,0:T(8,128)S(1)} custom-call(s32[27,48]{1,0:T(8,128)S(1)} %bitcast.6, s32[27,48]{1,0:T(8,128)S(1)} %bitcast.7, s32[48]{0:T(128)S(1)} %copy-done.4, bf16[192,48,128]{2,1,0:T(8,128)(2,1)S(1)} %gather_prolong.1.tile_ref, bf16[48,48,48]{2,1,0:T(8,128)(2,1)S(1)} %copy-done.1, bf16[48,27,48,48]{3,2,1,0:T(8,128)(2,1)} %blk_ref.1), custom_call_target="tpu_custom_call" | custom-call | flops 573308928 | bytes 20971520 | tf_op jit(solution)/shard_map/triple_products/pallas_call | solution.py:176
  42.8 32.1 %scatter_cols.1 = f32[432,288]{1,0:T(8,128)S(1)} custom-call(f32[21504,128]{1,0:T(8,128)S(1)} %triple_products.1.acc), custom_call_target="tpu_custom_call" | custom-call | tf_op jit(solution)/shard_map/scatter_cols/pallas_call | solution.py:310
  74.9 0.8 %copy.7 = f32[16,27,288]{2,0,1:T(8,128)} copy(f32[16,27,288]{2,0,1:T(8,128)S(1)} %bitcast.5) | data formatting | bytes 995328
Async XLA Ops:
  0.0 1.1 %copy-start = (bf16[48,48,48]{2,1,0:T(8,128)(2,1)S(1)}, bf16[48,48,48]{2,1,0:T(8,128)(2,1)}, u32[]{:S(2)}) copy-start(bf16[48,48,48]{2,1,0:T(8,128)(2,1)} %own_ref.1) | copy-start | bytes 663556
  12.9 1.1 %copy-start.1 = (bf16[48,48,48]{2,1,0:T(8,128)(2,1)S(1)}, bf16[48,48,48]{2,1,0:T(8,128)(2,1)}, u32[]{:S(2)}) copy-start(bf16[48,48,48]{2,1,0:T(8,128)(2,1)} %own_ref.1) | copy-start | bytes 663556
  13.9 0.7 copy-start.2
  14.6 0.7 copy-start.3
  15.4 0.7 copy-start.4
